TPU v7x, 256 devices: a whole 4x4x8 slice. The times are simulated.
256 devices in a mesh: samp: 32 (over z_hi, y, core), tp: 8 (over z_lo, x).
Axes of the slice: x: 4, y: 4, z: 8 (z_hi: 4, z_lo: 2; z = z_hi * 2 + z_lo), core: 2. Of those that a mesh axis runs over, the one named last changes fastest.
Arguments:
- queries: bfloat16 [12288, 32, 128], P('samp', 'tp'), may hold values from -9 to 9
- cache: bfloat16 [32, 1024, 8, 256], P('samp', None, 'tp'), may hold values from -6 to 6
- new_kv: bfloat16 [12288, 8, 256], P('samp', 'tp'), may hold values from -6 to 6
- slot_prompt: int32 [32], replicated, may hold values from 0 to 31, each once
- residual: bfloat16 [12288, 8192], P(('samp', 'tp')), may hold values from -60 to 60
- out_weight: bfloat16 [4096, 8192], P('tp'), may hold values from -0.5 to 0.5
- gain: float32 [8192], replicated, may hold values from 0.1 to 1.9
Outputs:
- hidden: bfloat16 [12288, 8192], P(('samp', 'tp'))
- normed: bfloat16 [12288, 8192], P(('samp', 'tp'))
Inputs may be any that keep to these rules, and one draw needn't show every extreme that they name: `slot_prompt`: every prompt stands in exactly one slot.
All inputs are finite; a program needn't handle non-finite values.
Results may differ from a plain program's by a relative error of at most 0.017.
Values may be sent and summed in bfloat16 or wider, within the bound.
A program may use at most 128 MiB of HBM per device.

v0:
```python
import jax
import jax.numpy as jnp
from jax import lax
from jax.sharding import PartitionSpec as P

STEPS = 3


def prefix_attend(query_grid, keys_values, head_size):
    score_scale = 1.0 / jnp.sqrt(jnp.float32(head_size))
    keys = keys_values[..., :head_size]
    values = keys_values[..., head_size:]
    score_form = "nsthgd,nlhd->nsthgl"
    value_form = "nsthgl,nlhd->nsthgd"
    scores = (
        jnp.einsum(score_form, query_grid, keys, preferred_element_type=jnp.float32) * score_scale
    )
    maximum = jnp.max(scores, -1)
    weights = jnp.exp(scores - maximum[..., None])
    denominator = jnp.sum(weights, -1)
    summed = jnp.einsum(
        value_form, weights.astype(jnp.bfloat16), values, preferred_element_type=jnp.float32
    )
    return (summed, maximum, denominator)


def combine_states(first, second):
    maximum = jnp.maximum(first[1], second[1])
    first_factor = jnp.exp(first[1] - maximum)
    second_factor = jnp.exp(second[1] - maximum)
    summed = first[0] * first_factor[..., None] + second[0] * second_factor[..., None]
    denominator = first[2] * first_factor + second[2] * second_factor
    return (summed, maximum, denominator)


def on_device(queries, cache, new_kv, slot_prompt, residual, out_weight, gain):
    row_total, heads_local, head_size = queries.shape
    kv_local = new_kv.shape[1]
    group_size = heads_local // kv_local
    prompt_count = slot_prompt.shape[0]
    samples = row_total // (prompt_count * STEPS)
    score_scale = 1.0 / jnp.sqrt(jnp.float32(head_size))
    query_grid = queries.reshape(prompt_count, samples, STEPS, kv_local, group_size, head_size)
    own_grid = new_kv.reshape(prompt_count, samples, STEPS, kv_local, 2 * head_size)
    own_scores = (
        jnp.einsum(
            "psthgd,psuhd->psthgu",
            query_grid,
            own_grid[..., :head_size],
            preferred_element_type=jnp.float32,
        )
        * score_scale
    )
    step_index = jnp.arange(STEPS)
    causal_mask = (step_index[None, :] <= step_index[:, None])[None, None, :, None, None, :]
    own_scores = jnp.where(causal_mask, own_scores, -jnp.inf)
    own_maximum = jnp.max(own_scores, -1)
    own_weights = jnp.exp(own_scores - own_maximum[..., None])
    own_denominator = jnp.sum(own_weights, -1)
    own_summed = jnp.einsum(
        "psthgu,psuhd->psthgd",
        own_weights.astype(jnp.bfloat16),
        own_grid[..., head_size:],
        preferred_element_type=jnp.float32,
    )
    own_state = (own_summed, own_maximum, own_denominator)
    selected = jnp.take(query_grid, slot_prompt, axis=0)
    fresh = prefix_attend(selected, lax.all_gather(cache, "samp", axis=0, tiled=True), head_size)
    previous = jax.tree.map(lambda whole: jnp.take(whole, slot_prompt, axis=0), own_state)
    merged = combine_states(previous, fresh)
    state = jax.tree.map(lambda whole, update: whole.at[slot_prompt].set(update), own_state, merged)
    attended = (state[0] / state[2][..., None]).astype(jnp.bfloat16)
    attended = attended.reshape(row_total, heads_local * head_size)
    projected = lax.psum_scatter(
        jnp.dot(attended, out_weight, preferred_element_type=jnp.float32).astype(jnp.bfloat16),
        "tp",
        scatter_dimension=0,
        tiled=True,
    ).astype(jnp.float32)
    hidden = (residual.astype(jnp.float32) + projected).astype(jnp.bfloat16)
    hidden_f = hidden.astype(jnp.float32)
    spread = jnp.sqrt(jnp.mean(hidden_f * hidden_f, -1) + 1e-05)
    normed = (hidden_f / spread[:, None] * gain[None, :]).astype(jnp.bfloat16)
    return (hidden, normed)


def solution(mesh):
    placed = (
        P("samp", "tp", None),
        P("samp", None, "tp", None),
        P("samp", "tp", None),
        P(),
        P(("samp", "tp"), None),
        P("tp", None),
        P(),
    )
    return jax.shard_map(
        on_device,
        mesh=mesh,
        in_specs=placed,
        out_specs=(P(("samp", "tp"), None), P(("samp", "tp"), None)),
        check_vma=False,
    )
```

profile of v0, /device:TPU:1, one launch (start us, length us, event | category | flops | bytes accessed | tf_op | source)
XLA Modules:
  0.0 251.4 jit_solution(12767036563586227293)
XLA Ops:
  7.2 0.7 all-gather.2.cloned.1.call-update
  8.0 1.0 reshape.118
  9.0 0.7 compare_select_fusion
  9.7 0.9 gather_fusion.1
  10.6 2.7 %fusion.51 = (f32[32,4,3,4]{3,2,1,0:T(4,128)S(1)}, f32[32,4,3,1,4,3]{4,5,2,1,0,3:T(4,128)S(1)}) fusion(bf16[32,4,3,4,128]{4,3,2,1,0:T(4,128)(2,1)S(1)} %bitcast.178, bf16[32,4,3,1,256]{4,2,1,0,3:T(4,128)(2,1)S(1)} %reshape.118, pred[3,3]{1,0:T(4,128)(4,1)S(1)} %iota_compare_fusion), kind=kOutput, calls=%fused_computation.69 | convolution fusion | flops 1191936 | bytes 549376 | tf_op jit(solution)/shard_map/psthgd,psuhd->psthgu/dot_general | solution.py:46
  13.3 0.7 gather_fusion.2
  14.0 0.7 fusion.31
  14.8 0.7 gather_fusion.3
  15.4 0.6 fusion.34
  16.1 1.9 gather_fusion
  17.9 109.6 %all-gather.2.cloned.1.call-done = bf16[32,1024,1,256]{3,1,2,0:T(8,128)(2,1)} async-done(((bf16[1,1024,1,256]{3,1,2,0:T(8,128)(2,1)}), bf16[32,1024,1,256]{3,1,2,0:T(8,128)(2,1)}) %all-gather.2.cloned.1.call-update) | async-done | bytes 16777232 | tf_op jit(solution)/shard_map/all_gather | solution.py:68
  127.6 9.3 %bitcast_reduce_fusion = (f32[32,4,3,4]{3,2,1,0:T(4,128)S(1)}, f32[32,4,3,4,1024]{4,3,2,1,0:T(4,128)}) fusion(bf16[32,1024,1,256]{3,1,0,2:T(8,128)(2,1)} %bitcast.181, bf16[32,4,3,4,128]{4,3,2,1,0:T(4,128)(2,1)S(1)} %gather_fusion.1, pred[32]{0:T(512)(128)(4,1)S(1)} %compare_and_fusion), kind=kOutput, calls=%fused_computation.12 | convolution fusion | flops 405993984 | bytes 15079456 | tf_op jit(solution)/shard_map/nsthgd,nlhd->nsthgl/dot_general | solution.py:16
  136.8 5.5 %fusion.3 = f32[32,4,3,4]{3,2,1,0:T(4,128)S(1)} fusion(f32[32,4,3,4,1024]{4,3,2,1,0:T(4,128)} %get-tuple-element.11, f32[32,4,3,4]{3,2,1,0:T(4,128)S(1)} %get-tuple-element.10), kind=kLoop, calls=%fused_computation.14 | loop fusion | flops 4717056 | bytes 6303744 | tf_op jit(solution)/shard_map/reduce_sum | solution.py:20
  142.3 0.3 fusion.44
  142.6 1.6 scatter_fusion.1
  144.3 0.1 copy.36
  144.3 0.1 copy.38
  144.4 7.4 %fusion.25 = f32[32,4,3,4,128]{4,3,2,1,0:T(4,128)S(1)} fusion(bf16[32,1024,1,256]{3,1,0,2:T(8,128)(2,1)} %bitcast.182, f32[32,4,3,4,1024]{4,3,2,1,0:T(4,128)} %get-tuple-element.11, f32[32,4,3,4]{3,2,1,0:T(4,128)S(1)} %get-tuple-element.10, f32[32,4,3,4,128]{4,3,2,1,0:T(4,128)} %gather_fusion, f32[32,4,3,4]{3,2,1,0:T(4,128)S(1)} %copy.38, ...), kind=kOutput, calls=%fused_computation.31 | convolution fusion | flops 408158208 | bytes 16271392 | tf_op jit(solution)/shard_map/nsthgl,nlhd->nsthgd/dot_general | solution.py:21
  151.8 1.7 scatter_fusion
  153.5 0.5 fusion.30
  154.0 8.8 %convolution_convert_fusion = bf16[384,8192]{1,0:T(8,128)(2,1)} fusion(bf16[512,8192]{1,0:T(8,128)(2,1)} %param.14, bf16[48,8,4,128]{3,2,1,0:T(4,128)(2,1)S(1)} %bitcast.180), kind=kOutput, calls=%fused_computation.6 | convolution fusion | flops 3224371200 | bytes 15073280 | tf_op jit(solution)/shard_map/dot_general | solution.py:75
  162.8 79.1 %reduce-scatter.2.cloned.1.call-done = bf16[48,8192]{1,0:T(8,128)(2,1)} async-done(((bf16[384,8192]{1,0:T(8,128)(2,1)}), bf16[48,8192]{1,0:T(8,128)(2,1)}) %reduce-scatter.2.cloned.1.call-update) | async-done | bytes 786448 | tf_op jit(solution)/shard_map/reduce_scatter | solution.py:74
  241.9 1.5 fusion.9
  243.5 1.1 fusion.11
  (20 shorter events, 0.3 us)
Async XLA Ops:
  7.2 2.5 copy-start
  7.2 10.7 %copy-start.4 = (s32[32]{0:T(128)S(1)}, s32[32]{0:T(128)}, u32[]{:S(2)}) copy-start(s32[32]{0:T(128)} %param.12) | copy-start | bytes 388
  7.2 120.4 %all-gather.2.cloned.1.call-start = ((), (), s32[]{:S(2)}) async-start(), calls=%async_computation.1 | async-start | bytes 17301504 | tf_op jit(solution)/shard_map/all_gather | solution.py:68
  7.9 234.0 %reduce-scatter.2.cloned.1.call-start = ((), (), s32[]{:S(2)}) async-start(), calls=%async_computation.2 | async-start | bytes 7077888 | tf_op jit(solution)/shard_map/reduce_scatter | solution.py:74
  162.7 79.2 %copy-start.2 = (bf16[48,8192]{1,0:T(8,128)(2,1)S(1)}, bf16[48,8192]{1,0:T(8,128)(2,1)}, u32[]{:S(2)}) copy-start(bf16[48,8192]{1,0:T(8,128)(2,1)} %param.13) | copy-start | bytes 2359300
  162.7 80.7 %copy-start.3 = (f32[8192]{0:T(1024)S(1)}, f32[8192]{0:T(1024)}, u32[]{:S(2)}) copy-start(f32[8192]{0:T(1024)} %param.15) | copy-start | bytes 98308
  243.4 1.2 copy-start.1
Sparse Core Ops, SparseCore 0:
  10.6 116.9 all-gather.1
  162.9 78.9 reduce-scatter.1
where the time goes:
time: 252 us; the launch traced here: 251 us
  waiting for transfers between devices  189 us (75%)
  matrix products  28.7 us (11%)
  between operations  14.2 us (6%)
  other arithmetic  10.3 us (4%)
  local copies, waits for them, and re-layouts  8.7 us (3%)
    all_gather x1, waiting for transfers between devices, on_device(): lax.all_gather(cache, 'samp', axis=0, tiled=True)  110 us
    reduce_scatter x1, waiting for transfers between devices, on_device(): lax.psum_scatter(jnp.dot(attended, out_weight, preferred_element_type=jnp...  79.1 us
    dot_general x1, matrix products, prefix_attend(): jnp.einsum(score_form, query_grid, keys, preferred_element_type=jnp.float32)  9.28 us
    dot_general x1, matrix products, on_device(): jnp.dot(attended, out_weight, preferred_element_type=jnp.float32)  8.76 us
    dot_general x1, matrix products, prefix_attend(): jnp.einsum(value_form, weights.astype(jnp.bfloat16), values, preferred_el...  7.38 us
    reduce_sum x1, other arithmetic, prefix_attend(): denominator = jnp.sum(weights, -1)  5.49 us
  transfers between devices with their start and end apart: 2, of which 2 were waited for; matrix products, arithmetic and copies ran while one was open for 4% of the time, Pallas kernels for 0%

commit v1 on v0

v1 whole, which is shorter than its diff:
```python
import math

import jax
import jax.numpy as jnp
from jax import lax
from jax.experimental import pallas as pl
from jax.experimental.pallas import tpu as pltpu
from jax.sharding import PartitionSpec as P

STEPS = 3
SOURCES_PER_BLOCK = 8


def attend_kernel(group_size, sent_ref, cache_ref, out_ref):
    sources, width, head_size = sent_ref.shape
    query_rows = out_ref.shape[1]
    own_rows = width - query_rows
    factor = math.log2(math.e) / math.sqrt(head_size)
    nt = (((1,), (1,)), ((), ()))
    nn = (((1,), (0,)), ((), ()))
    query = sent_ref[:, :query_rows, :].reshape(sources * query_rows, head_size)
    own = sent_ref[:, query_rows:, :].astype(jnp.float32)
    own = own.reshape(sources * own_rows, head_size).astype(jnp.bfloat16)
    total_own = sources * own_rows
    at = lax.broadcasted_iota(jnp.int32, (total_own, total_own), 0)
    taken = lax.broadcasted_iota(jnp.int32, (total_own, total_own), 1)
    move = jnp.where((taken == at + 1) & (lax.rem(at, 2) == 0), 1.0, 0.0).astype(jnp.bfloat16)
    own_value = lax.dot_general(move, own, nn, preferred_element_type=jnp.float32)
    own_value = own_value.astype(jnp.bfloat16)
    prompt_score = lax.dot_general(
        query, cache_ref[:, :head_size], nt, preferred_element_type=jnp.float32
    )
    own_score = lax.dot_general(query, own, nt, preferred_element_type=jnp.float32)
    row = lax.broadcasted_iota(jnp.int32, own_score.shape, 0) // group_size
    column = lax.broadcasted_iota(jnp.int32, own_score.shape, 1)
    key = column // 2
    seen = (lax.rem(column, 2) == 0) & (key <= row) & (key >= row - lax.rem(row, STEPS))
    own_score = jnp.where(seen, own_score, -jnp.inf)
    maximum = jnp.maximum(
        jnp.max(prompt_score, -1, keepdims=True), jnp.max(own_score, -1, keepdims=True)
    )
    shift = maximum * factor
    prompt_weight = jnp.exp2(prompt_score * factor - shift)
    own_weight = jnp.exp2(own_score * factor - shift)
    denominator = jnp.sum(prompt_weight, -1, keepdims=True) + jnp.sum(
        own_weight, -1, keepdims=True
    )
    summed = lax.dot_general(
        prompt_weight.astype(jnp.bfloat16),
        cache_ref[:, head_size:],
        nn,
        preferred_element_type=jnp.float32,
    )
    summed = summed + lax.dot_general(
        own_weight.astype(jnp.bfloat16), own_value, nn, preferred_element_type=jnp.float32
    )
    attended = (summed / denominator).astype(jnp.bfloat16)
    out_ref[...] = attended.reshape(sources, query_rows, head_size)


def attend(sent, cache, query_rows, group_size):
    sources, width, head_size = sent.shape
    block = min(SOURCES_PER_BLOCK, sources)
    return pl.pallas_call(
        lambda *refs: attend_kernel(group_size, *refs),
        grid=(sources // block,),
        in_specs=[
            pl.BlockSpec((block, width, head_size), lambda i: (i, 0, 0)),
            pl.BlockSpec(cache.shape, lambda i: (0, 0)),
        ],
        out_specs=pl.BlockSpec((block, query_rows, head_size), lambda i: (i, 0, 0)),
        out_shape=jax.ShapeDtypeStruct((sources, query_rows, head_size), jnp.bfloat16),
        compiler_params=pltpu.CompilerParams(vmem_limit_bytes=40 * 2**20),
    )(sent, cache)


def on_device(queries, cache, new_kv, slot_prompt, residual, out_weight, gain):
    row_total, heads_local, head_size = queries.shape
    group_size = heads_local // new_kv.shape[1]
    prompt_count = slot_prompt.shape[0]
    rows = row_total // prompt_count
    packed = jnp.concatenate(
        [
            queries.reshape(prompt_count, rows * heads_local, head_size),
            new_kv.reshape(prompt_count, rows * 2, head_size),
        ],
        axis=1,
    )
    sent = jnp.take(packed, slot_prompt, axis=0)
    sent = lax.all_to_all(sent, "samp", 0, 0, tiled=True)
    attended = attend(sent, cache.reshape(cache.shape[1], 2 * head_size), rows * heads_local, group_size)
    attended = lax.all_to_all(attended, "samp", 0, 0, tiled=True)
    slot_of = jnp.zeros_like(slot_prompt).at[slot_prompt].set(jnp.arange(prompt_count, dtype=jnp.int32))
    attended = jnp.take(attended, slot_of, axis=0).reshape(row_total, heads_local * head_size)
    projected = lax.psum_scatter(
        jnp.dot(attended, out_weight, preferred_element_type=jnp.float32).astype(jnp.bfloat16),
        "tp",
        scatter_dimension=0,
        tiled=True,
    ).astype(jnp.float32)
    hidden = (residual.astype(jnp.float32) + projected).astype(jnp.bfloat16)
    hidden_f = hidden.astype(jnp.float32)
    spread = jnp.sqrt(jnp.mean(hidden_f * hidden_f, -1) + 1e-05)
    normed = (hidden_f / spread[:, None] * gain[None, :]).astype(jnp.bfloat16)
    return (hidden, normed)


def solution(mesh):
    placed = (
        P("samp", "tp", None),
        P("samp", None, "tp", None),
        P("samp", "tp", None),
        P(),
        P(("samp", "tp"), None),
        P("tp", None),
        P(),
    )
    return jax.shard_map(
        on_device,
        mesh=mesh,
        in_specs=placed,
        out_specs=(P(("samp", "tp"), None), P(("samp", "tp"), None)),
        check_vma=False,
    )
```

time: 252 us -> 161 us (0.64)
  waiting for transfers between devices: 189 us -> 86.4 us
  blocking collectives: 0 us -> 31.7 us
  matrix products: 28.7 us -> 8.72 us
  Pallas kernels: 0 us -> 6.36 us
  local copies, waits for them, and re-layouts: 8.7 us -> 3.23 us
  other arithmetic: 10.3 us -> 5.28 us
  starting transfers between devices: 0.08 us -> 4.93 us
    all_gather x1 -> x0, waiting for transfers between devices: 110 us -> none  [on_device(): lax.all_gather(cache, 'samp', axis=0, tiled=True)]
    all_to_all x0 -> x1, blocking collectives: none -> 31.7 us  [on_device(): sent = lax.all_to_all(sent, 'samp', 0, 0, tiled=True)]
    dot_general x4 -> x0, matrix products: 19.9 us -> none  [the longest x1 9.28 us: prefix_attend(): jnp.einsum(score_form, query_grid, keys, preferred_element_type=jnp.float32)]
    all_to_all x0 -> x1, waiting for transfers between devices: none -> 14.9 us  [on_device(): attended = lax.all_to_all(attended, 'samp', 0, 0, tiled=True)]
    reduce_scatter x1, waiting for transfers between devices: 79.1 us -> 71.5 us  [on_device(): lax.psum_scatter(jnp.dot(attended, out_weight, preferred_element_type=jnp...]
    pallas_call x0 -> x1, Pallas kernels: none -> 6.36 us  [attend(): pl.pallas_call(lambda *refs: attend_kernel(group_size, *refs), grid=(sour...]
    reduce_sum x2 -> x0, other arithmetic: 6.22 us -> none  [the longest x1 5.49 us: prefix_attend(): denominator = jnp.sum(weights, -1)]
    all_to_all x0 -> x1, starting transfers between devices: none -> 4.89 us  [on_device(): attended = lax.all_to_all(attended, 'samp', 0, 0, tiled=True)]
  transfers between devices with their start and end apart: 2 -> 2, of which waited for: 2 -> 2; matrix products, arithmetic and copies ran while one was open for 4% -> 0% of each run, Pallas kernels for 0% -> 0%
where the time goes in v1:
time: 161 us
  waiting for transfers between devices  86.4 us (54%)
  blocking collectives  31.7 us (20%)
  between operations  14.2 us (9%)
  matrix products  8.72 us (5%)
  Pallas kernels  6.36 us (4%)
  other arithmetic  5.28 us (3%)
  starting transfers between devices  4.93 us (3%)
  local copies, waits for them, and re-layouts  3.23 us (2%)
    reduce_scatter x1, waiting for transfers between devices, on_device(): lax.psum_scatter(jnp.dot(attended, out_weight, preferred_element_type=jnp...  71.5 us
    all_to_all x1, blocking collectives, on_device(): sent = lax.all_to_all(sent, 'samp', 0, 0, tiled=True)  31.7 us
    all_to_all x1, waiting for transfers between devices, on_device(): attended = lax.all_to_all(attended, 'samp', 0, 0, tiled=True)  14.9 us
    dot_general x1, matrix products, on_device(): jnp.dot(attended, out_weight, preferred_element_type=jnp.float32)  8.72 us
    pallas_call x1, Pallas kernels, attend(): pl.pallas_call(lambda *refs: attend_kernel(group_size, *refs), grid=(sour...  6.36 us
    all_to_all x1, starting transfers between devices, on_device(): attended = lax.all_to_all(attended, 'samp', 0, 0, tiled=True)  4.89 us
  transfers between devices with their start and end apart: 2, of which 2 were waited for; matrix products, arithmetic and copies ran while one was open for 0% of the time, Pallas kernels for 0%

profile of v1, /device:TPU:1, one launch (start us, length us, event | category | flops | bytes accessed | tf_op | source)
XLA Modules:
  0.0 160.8 jit_solution(2493979677953190389)
XLA Ops:
  7.2 0.7 compare_select_fusion.1
  7.8 0.7 compare_and_fusion
  8.5 1.0 reshape.35
  9.5 1.0 pad_maximum_fusion
  10.5 0.0 copy-start
  10.6 0.7 gather_fusion
  11.2 0.1 broadcast_select_fusion
  11.4 31.7 %all_to_all.10.refs_0_ = bf16[32,72,128]{2,1,0:T(8,128)(2,1)S(1)} all-to-all(bf16[32,72,128]{2,1,0:T(8,128)(2,1)S(1)} %broadcast_select_fusion), channel_id=1, replica_groups=mesh['samp'=32,'tp'=8] {'samp'}, dimensions={0} | all-to-all | bytes 1179648 | tf_op jit(solution)/shard_map/all_to_all | solution.py:90
  43.1 0.0 copy-done
  43.1 6.4 %shard_map.86 = bf16[32,48,128]{2,1,0:T(8,128)(2,1)} custom-call(bf16[32,72,128]{2,1,0:T(8,128)(2,1)S(1)} %all_to_all.10.refs_0_, bf16[1024,256]{1,0:T(8,128)(2,1)S(1)} %bitcast.7), custom_call_target="tpu_custom_call" | custom-call | tf_op jit(solution)/shard_map/pallas_call | solution.py:64
  49.4 4.9 %all-to-all-start.1 = ((bf16[32,48,128]{2,1,0:T(8,128)(2,1)}), bf16[32,48,128]{2,1,0:T(8,128)(2,1)S(1)}, u32[]{:S(2)}, u32[]{:S(2)}) async-start(bf16[32,48,128]{2,1,0:T(8,128)(2,1)} %shard_map.86), calls=%async_computation.1 | async-start | bytes 786432 | tf_op jit(solution)/shard_map/all_to_all | solution.py:92
  54.3 0.0 reduce-scatter.2.cloned.1.call-start
  54.4 0.7 scatter_custom_fusion
  55.1 14.9 %all-to-all-done.1 = bf16[32,48,128]{2,1,0:T(8,128)(2,1)S(1)} async-done(((bf16[32,48,128]{2,1,0:T(8,128)(2,1)}), bf16[32,48,128]{2,1,0:T(8,128)(2,1)S(1)}, u32[]{:S(2)}, u32[]{:S(2)}) %all-to-all-start.1) | async-done | bytes 393248 | tf_op jit(solution)/shard_map/all_to_all | solution.py:92
  70.0 0.6 gather_fusion.1
  70.6 0.1 broadcast_select_fusion.1
  70.8 0.2 select_n.26
  71.0 8.7 %convolution_convert_fusion = bf16[384,8192]{1,0:T(8,128)(2,1)} fusion(bf16[384,512]{1,0:T(8,128)(2,1)S(1)} %select_n.26, bf16[512,8192]{1,0:T(8,128)(2,1)} %param.12), kind=kOutput, calls=%fused_computation.3 | convolution fusion | flops 3224371200 | bytes 15073280 | tf_op jit(solution)/shard_map/dot_general | solution.py:96
  79.7 0.0 reduce-scatter.2.cloned.1.call-update
  79.8 0.0 copy-start.3
  79.8 71.5 %reduce-scatter.2.cloned.1.call-done = bf16[48,8192]{1,0:T(8,128)(2,1)} async-done(((bf16[384,8192]{1,0:T(8,128)(2,1)}), bf16[48,8192]{1,0:T(8,128)(2,1)}) %reduce-scatter.2.cloned.1.call-update) | async-done | bytes 786448 | tf_op jit(solution)/shard_map/reduce_scatter | solution.py:95
  151.2 1.5 fusion
  152.7 0.0 copy-start.1
  152.8 1.1 fusion.2
  (10 shorter events, 0.0 us)
Async XLA Ops:
  10.5 32.5 %copy-start = (bf16[1,1024,1,256]{3,1,2,0:T(8,128)(2,1)S(1)}, bf16[1,1024,1,256]{3,1,2,0:T(8,128)(2,1)}, u32[]{:S(2)}) copy-start(bf16[1,1024,1,256]{3,1,2,0:T(8,128)(2,1)} %param.8) | copy-start | bytes 1572868
  49.4 20.6 %all-to-all-start.1 = ((bf16[32,48,128]{2,1,0:T(8,128)(2,1)}), bf16[32,48,128]{2,1,0:T(8,128)(2,1)S(1)}, u32[]{:S(2)}, u32[]{:S(2)}) async-start(bf16[32,48,128]{2,1,0:T(8,128)(2,1)} %shard_map.86), calls=%async_computation.1 | async-start | bytes 786432 | tf_op jit(solution)/shard_map/all_to_all | solution.py:92
  54.3 96.9 %reduce-scatter.2.cloned.1.call-start = ((), (), s32[]{:S(2)}) async-start(), calls=%async_computation.3 | async-start | bytes 7077888 | tf_op jit(solution)/shard_map/reduce_scatter | solution.py:95
  79.7 71.5 %copy-start.2 = (bf16[48,8192]{1,0:T(8,128)(2,1)S(1)}, bf16[48,8192]{1,0:T(8,128)(2,1)}, u32[]{:S(2)}) copy-start(bf16[48,8192]{1,0:T(8,128)(2,1)} %param.11) | copy-start | bytes 2359300
  79.8 73.0 %copy-start.3 = (f32[8192]{0:T(1024)S(1)}, f32[8192]{0:T(1024)}, u32[]{:S(2)}) copy-start(f32[8192]{0:T(1024)} %param.13) | copy-start | bytes 98308
  152.7 1.2 copy-start.1
Sparse Core Ops, SparseCore 0:
  79.9 71.3 reduce-scatter.1

commit v2 on v1

--- a/solution.py
+++ b/solution.py
@@ -74,6 +74,262 @@
     )(sent, cache)
 
 
+RING = 4
+RING_FIRST = 5
+PAIR_FIRST = 3
+
+
+def project_kernel(
+    attended_ref,
+    weight_hbm,
+    out_ref,
+    weight,
+    weight_sem,
+    xp,
+    xr,
+    xq,
+    zp,
+    zq,
+    zr,
+    xr_send,
+    xr_recv,
+    xq_send,
+    xq_recv,
+    zq_send,
+    zq_recv,
+    zr_send,
+    zr_recv,
+):
+    rows = out_ref.shape[0]
+    width = weight.shape[2]
+    chunks = weight.shape[0]
+    here = lax.axis_index("tp")
+    x = lax.rem(here, RING)
+    z = here // RING
+    other = 1 - z
+
+    def ring_device(way):
+        step = 1 if way == 0 else RING - 1
+        return {"tp": z * RING + lax.rem(x + step, RING)}
+
+    pair_device = {"tp": other * RING + x}
+
+    def block(way, step):
+        ahead = 2 * RING - 1 - step if way == 0 else 1 + step
+        return lax.rem(x + ahead, RING)
+
+    def ring_chunk(k, way):
+        return 2 * k + way
+
+    def pair_chunk(k, way):
+        return 2 * RING_FIRST + 2 * k + way
+
+    def fetch(chunk):
+        return pltpu.make_async_copy(
+            weight_hbm.at[:, pl.ds(chunk * width, width)], weight.at[chunk], weight_sem.at[chunk]
+        )
+
+    def remote(src, dst, send, recv, device):
+        return pltpu.make_async_remote_copy(
+            src_ref=src,
+            dst_ref=dst,
+            send_sem=send,
+            recv_sem=recv,
+            device_id=device,
+            device_id_type=pl.DeviceIdType.MESH,
+        )
+
+    def ring_copy(k, way, step):
+        return remote(
+            xp.at[way, k, block(way, step)],
+            xr.at[way, k, step],
+            xr_send.at[way, k, step],
+            xr_recv.at[way, k, step],
+            ring_device(way),
+        )
+
+    def ring_pair_copy(k, way):
+        return remote(
+            xp.at[way, k, x, other],
+            xq.at[way, k],
+            xq_send.at[way, k],
+            xq_recv.at[way, k],
+            pair_device,
+        )
+
+    def pair_copy(k, way):
+        return remote(
+            zp.at[way, k, other],
+            zq.at[way, k],
+            zq_send.at[way, k],
+            zq_recv.at[way, k],
+            pair_device,
+        )
+
+    def pair_ring_copy(k, way, step):
+        return remote(
+            zp.at[way, k, z, block(way, step)],
+            zr.at[way, k, step],
+            zr_send.at[way, k, step],
+            zr_recv.at[way, k, step],
+            ring_device(way),
+        )
+
+    def multiply(chunk):
+        fetch(chunk).wait()
+        product = jnp.dot(
+            attended_ref[...], weight[chunk], preferred_element_type=jnp.float32
+        )
+        return product.astype(jnp.bfloat16)
+
+    def start_ring(k):
+        for way in range(2):
+            product = multiply(ring_chunk(k, way))
+            for j in range(2 * RING):
+                xp[way, k, j % RING, j // RING] = product[j * rows : (j + 1) * rows]
+            ring_copy(k, way, 0).start()
+
+    def start_pair(k):
+        for way in range(2):
+            product = multiply(pair_chunk(k, way))
+            for j in range(2 * RING):
+                zp[way, k, j // RING, j % RING] = product[j * rows : (j + 1) * rows]
+            pair_copy(k, way).start()
+
+    def wide(value):
+        return value.astype(jnp.float32)
+
+    def ring_step(k, step):
+        for way in range(2):
+            ring_copy(k, way, step).wait_recv()
+            at = block(way, step + 1)
+            xp[way, k, at] = (wide(xp[way, k, at]) + wide(xr[way, k, step])).astype(jnp.bfloat16)
+            if step < RING - 2:
+                ring_copy(k, way, step + 1).start()
+            else:
+                ring_pair_copy(k, way).start()
+
+    def ring_end(k):
+        for way in range(2):
+            ring_pair_copy(k, way).wait_recv()
+            columns = pl.ds(ring_chunk(k, way) * width, width)
+            out_ref[:, columns] = (wide(xp[way, k, x, z]) + wide(xq[way, k])).astype(jnp.bfloat16)
+
+    def pair_step(k):
+        for way in range(2):
+            pair_copy(k, way).wait_recv()
+            at = block(way, 0)
+            zp[way, k, z, at] = (wide(zp[way, k, z, at]) + wide(zq[way, k, at])).astype(
+                jnp.bfloat16
+            )
+            pair_ring_copy(k, way, 0).start()
+
+    def pair_ring_step(k, step):
+        for way in range(2):
+            pair_ring_copy(k, way, step).wait_recv()
+            at = block(way, step + 1)
+            total = wide(zp[way, k, z, at]) + wide(zq[way, k, at]) + wide(zr[way, k, step])
+            if step < RING - 2:
+                zp[way, k, z, at] = total.astype(jnp.bfloat16)
+                pair_ring_copy(k, way, step + 1).start()
+            else:
+                columns = pl.ds(pair_chunk(k, way) * width, width)
+                out_ref[:, columns] = total.astype(jnp.bfloat16)
+
+    order = []
+    for k in range(max(RING_FIRST, PAIR_FIRST)):
+        order += [pair_chunk(k, way) for way in range(2)] if k < PAIR_FIRST else []
+        order += [ring_chunk(k, way) for way in range(2)] if k < RING_FIRST else []
+    for chunk in order:
+        fetch(chunk).start()
+    barrier = pltpu.get_barrier_semaphore()
+    for device in (ring_device(0), ring_device(1), pair_device):
+        pl.semaphore_signal(
+            barrier, inc=1, device_id=device, device_id_type=pl.DeviceIdType.MESH
+        )
+    pl.semaphore_wait(barrier, 3)
+
+    for k in range(max(RING_FIRST, PAIR_FIRST)):
+        if k < PAIR_FIRST:
+            start_pair(k)
+        if k < RING_FIRST:
+            start_ring(k)
+    steps = []
+    for k in range(RING_FIRST):
+        for step in range(RING - 1):
+            steps.append((step + (k + 1) / RING_FIRST, 0, k, step))
+        steps.append((3.2 + (k + 1) * 1.0 / RING_FIRST, 1, k, 0))
+    for k in range(PAIR_FIRST):
+        arrival = 3.0 * (k + 1) / PAIR_FIRST
+        steps.append((arrival, 2, k, 0))
+        for step in range(RING - 1):
+            steps.append((arrival + 0.45 * (step + 1), 3, k, step))
+    for _, kind, k, step in sorted(steps):
+        if kind == 0:
+            ring_step(k, step)
+        elif kind == 1:
+            ring_end(k)
+        elif kind == 2:
+            pair_step(k)
+        else:
+            pair_ring_step(k, step)
+    for way in range(2):
+        for k in range(RING_FIRST):
+            for step in range(RING - 1):
+                ring_copy(k, way, step).wait_send()
+            ring_pair_copy(k, way).wait_send()
+        for k in range(PAIR_FIRST):
+            pair_copy(k, way).wait_send()
+            for step in range(RING - 1):
+                pair_ring_copy(k, way, step).wait_send()
+
+
+def project(attended, out_weight):
+    total, depth = attended.shape
+    columns = out_weight.shape[1]
+    rows = total // (2 * RING)
+    chunks = 2 * (RING_FIRST + PAIR_FIRST)
+    width = columns // chunks
+    steps = RING - 1
+    dma = pltpu.SemaphoreType.DMA
+    held = jnp.bfloat16
+    return pl.pallas_call(
+        project_kernel,
+        in_specs=[
+            pl.BlockSpec(memory_space=pltpu.VMEM),
+            pl.BlockSpec(memory_space=pl.ANY),
+        ],
+        out_specs=pl.BlockSpec(memory_space=pltpu.VMEM),
+        out_shape=jax.ShapeDtypeStruct((rows, columns), held),
+        scratch_shapes=[
+            pltpu.VMEM((chunks, depth, width), held),
+            dma((chunks,)),
+            pltpu.VMEM((2, RING_FIRST, RING, 2, rows, width), held),
+            pltpu.VMEM((2, RING_FIRST, steps, 2, rows, width), held),
+            pltpu.VMEM((2, RING_FIRST, rows, width), held),
+            pltpu.VMEM((2, PAIR_FIRST, 2, RING, rows, width), held),
+            pltpu.VMEM((2, PAIR_FIRST, RING, rows, width), held),
+            pltpu.VMEM((2, PAIR_FIRST, steps, rows, width), held),
+            dma((2, RING_FIRST, steps)),
+            dma((2, RING_FIRST, steps)),
+            dma((2, RING_FIRST)),
+            dma((2, RING_FIRST)),
+            dma((2, PAIR_FIRST)),
+            dma((2, PAIR_FIRST)),
+            dma((2, PAIR_FIRST, steps)),
+            dma((2, PAIR_FIRST, steps)),
+        ],
+        compiler_params=pltpu.CompilerParams(
+            collective_id=0, has_side_effects=True, vmem_limit_bytes=48 * 2**20
+        ),
+        cost_estimate=pl.CostEstimate(
+            flops=2 * total * depth * columns,
+            bytes_accessed=2 * (depth * columns + total * depth + rows * columns),
+            transcendentals=0,
+        ),
+    )(attended, out_weight)
+
+
 def on_device(queries, cache, new_kv, slot_prompt, residual, out_weight, gain):
     row_total, heads_local, head_size = queries.shape
     group_size = heads_local // new_kv.shape[1]
@@ -92,12 +348,7 @@
     attended = lax.all_to_all(attended, "samp", 0, 0, tiled=True)
     slot_of = jnp.zeros_like(slot_prompt).at[slot_prompt].set(jnp.arange(prompt_count, dtype=jnp.int32))
     attended = jnp.take(attended, slot_of, axis=0).reshape(row_total, heads_local * head_size)
-    projected = lax.psum_scatter(
-        jnp.dot(attended, out_weight, preferred_element_type=jnp.float32).astype(jnp.bfloat16),
-        "tp",
-        scatter_dimension=0,
-        tiled=True,
-    ).astype(jnp.float32)
+    projected = project(attended, out_weight).astype(jnp.float32)
     hidden = (residual.astype(jnp.float32) + projected).astype(jnp.bfloat16)
     hidden_f = hidden.astype(jnp.float32)
     spread = jnp.sqrt(jnp.mean(hidden_f * hidden_f, -1) + 1e-05)

time: 161 us -> 123 us (0.76); the launches traced: 161 us -> 121 us
  waiting for transfers between devices: 86.4 us -> 15 us
  Pallas kernels: 6.36 us -> 60.7 us
  between operations: 14.2 us -> 0.77 us
  matrix products: 8.72 us -> 0 us
    reduce_scatter x1 -> x0, waiting for transfers between devices: 71.5 us -> none  [on_device(): lax.psum_scatter(jnp.dot(attended, out_weight, preferred_element_type=jnp...]
    pallas_call x0 -> x1, Pallas kernels: none -> 54.4 us  [project(): pl.pallas_call(project_kernel, in_specs=[pl.BlockSpec(memory_space=pltpu....]
    dot_general x1 -> x0, matrix products: 8.72 us -> none  [on_device(): jnp.dot(attended, out_weight, preferred_element_type=jnp.float32)]
  transfers between devices with their start and end apart: 2 -> 1, of which waited for: 2 -> 1; matrix products, arithmetic and copies ran while one was open for 0% -> 1% of each run, Pallas kernels for 0% -> 0%
where the time goes in v2:
time: 123 us; the launch traced here: 121 us
  Pallas kernels  60.7 us (49%)
  blocking collectives  31.7 us (26%)
  waiting for transfers between devices  15 us (12%)
  starting transfers between devices  4.89 us (4%)
  other arithmetic  4.14 us (3%)
  local copies, waits for them, and re-layouts  3.57 us (3%)
    pallas_call x1, Pallas kernels, project(): pl.pallas_call(project_kernel, in_specs=[pl.BlockSpec(memory_space=pltpu....  54.4 us
    all_to_all x1, blocking collectives, on_device(): sent = lax.all_to_all(sent, 'samp', 0, 0, tiled=True)  31.7 us
    all_to_all x1, waiting for transfers between devices, on_device(): attended = lax.all_to_all(attended, 'samp', 0, 0, tiled=True)  15 us
    pallas_call x1, Pallas kernels, attend(): pl.pallas_call(lambda *refs: attend_kernel(group_size, *refs), grid=(sour...  6.32 us
    all_to_all x1, starting transfers between devices, on_device(): attended = lax.all_to_all(attended, 'samp', 0, 0, tiled=True)  4.89 us
  transfers between devices with their start and end apart: 1, of which 1 were waited for; matrix products, arithmetic and copies ran while one was open for 1% of the time, Pallas kernels for 0%

profile of v2, /device:TPU:1, one launch (start us, length us, event | category | flops | bytes accessed | tf_op | source)
XLA Modules:
  0.0 120.8 jit_solution(17078785403839051043)
XLA Ops:
  0.6 0.7 compare_select_fusion.1
  1.3 0.7 compare_and_fusion
  2.0 1.0 reshape.35
  3.0 1.0 pad_maximum_fusion
  4.0 0.0 copy-start
  4.0 0.7 gather_fusion
  4.7 0.1 broadcast_select_fusion
  4.8 31.7 %all_to_all.10.refs_0_ = bf16[32,72,128]{2,1,0:T(8,128)(2,1)S(1)} all-to-all(bf16[32,72,128]{2,1,0:T(8,128)(2,1)S(1)} %broadcast_select_fusion), channel_id=1, replica_groups=mesh['samp'=32,'tp'=8] {'samp'}, dimensions={0} | all-to-all | bytes 1179648 | tf_op jit(solution)/shard_map/all_to_all | solution.py:346
  36.5 0.0 copy-done
  36.5 6.3 %shard_map.86 = bf16[32,48,128]{2,1,0:T(8,128)(2,1)} custom-call(bf16[32,72,128]{2,1,0:T(8,128)(2,1)S(1)} %all_to_all.10.refs_0_, bf16[1024,256]{1,0:T(8,128)(2,1)S(1)} %bitcast.5), custom_call_target="tpu_custom_call" | custom-call | tf_op jit(solution)/shard_map/pallas_call | solution.py:64
  42.9 4.9 %all-to-all-start.1 = ((bf16[32,48,128]{2,1,0:T(8,128)(2,1)}), bf16[32,48,128]{2,1,0:T(8,128)(2,1)S(1)}, u32[]{:S(2)}, u32[]{:S(2)}) async-start(bf16[32,48,128]{2,1,0:T(8,128)(2,1)} %shard_map.86), calls=%async_computation.1 | async-start | bytes 786432 | tf_op jit(solution)/shard_map/all_to_all | solution.py:348
  47.8 0.7 scatter_custom_fusion
  48.5 15.0 %all-to-all-done.1 = bf16[32,48,128]{2,1,0:T(8,128)(2,1)S(1)} async-done(((bf16[32,48,128]{2,1,0:T(8,128)(2,1)}), bf16[32,48,128]{2,1,0:T(8,128)(2,1)S(1)}, u32[]{:S(2)}, u32[]{:S(2)}) %all-to-all-start.1) | async-done | bytes 393248 | tf_op jit(solution)/shard_map/all_to_all | solution.py:348
  63.4 0.6 gather_fusion.1
  64.1 0.1 broadcast_select_fusion.1
  64.2 0.2 select_n.26.attended_ref
  64.4 0.0 copy-start.2
  64.4 54.4 %shard_map.87 = bf16[48,8192]{1,0:T(8,128)(2,1)S(1)} custom-call(bf16[384,512]{1,0:T(8,128)(2,1)S(1)} %select_n.26.attended_ref, bf16[512,8192]{1,0:T(8,128)(2,1)} %weight_hbm.1), custom_call_target="tpu_custom_call" | custom-call | flops 3221225472 | bytes 9568256 | tf_op jit(solution)/shard_map/pallas_call | solution.py:296
  118.8 0.0 copy-done.2
  118.9 0.0 copy-start.3
  118.9 0.4 fusion
  119.2 0.0 copy-start.1
  119.3 0.3 copy-done.3
  119.6 1.1 fusion.2
  (7 shorter events, 0.0 us)
Async XLA Ops:
  4.0 32.5 %copy-start = (bf16[1,1024,1,256]{3,1,2,0:T(8,128)(2,1)S(1)}, bf16[1,1024,1,256]{3,1,2,0:T(8,128)(2,1)}, u32[]{:S(2)}) copy-start(bf16[1,1024,1,256]{3,1,2,0:T(8,128)(2,1)} %param.8) | copy-start | bytes 1572868
  42.9 20.6 %all-to-all-start.1 = ((bf16[32,48,128]{2,1,0:T(8,128)(2,1)}), bf16[32,48,128]{2,1,0:T(8,128)(2,1)S(1)}, u32[]{:S(2)}, u32[]{:S(2)}) async-start(bf16[32,48,128]{2,1,0:T(8,128)(2,1)} %shard_map.86), calls=%async_computation.1 | async-start | bytes 786432 | tf_op jit(solution)/shard_map/all_to_all | solution.py:348
  64.4 54.4 %copy-start.2 = (bf16[48,8192]{1,0:T(8,128)(2,1)S(1)}, bf16[48,8192]{1,0:T(8,128)(2,1)}, u32[]{:S(2)}) copy-start(bf16[48,8192]{1,0:T(8,128)(2,1)} %param.11) | copy-start | bytes 2359300
  118.9 0.8 copy-start.3
  119.2 1.5 %copy-start.1 = (bf16[48,8192]{1,0:T(8,128)(2,1)}, bf16[48,8192]{1,0:T(8,128)(2,1)S(1)}, u32[]{:S(2)}) copy-start(bf16[48,8192]{1,0:T(8,128)(2,1)S(1)} %get-tuple-element.3) | copy-start | bytes 2359300

commit v3 on v2

--- a/solution.py
+++ b/solution.py
@@ -1,3 +1,4 @@
+import functools
 import math
 
 import jax
@@ -8,70 +9,227 @@
 from jax.sharding import PartitionSpec as P
 
 STEPS = 3
-SOURCES_PER_BLOCK = 8
-
-
-def attend_kernel(group_size, sent_ref, cache_ref, out_ref):
-    sources, width, head_size = sent_ref.shape
-    query_rows = out_ref.shape[1]
-    own_rows = width - query_rows
+Z_HI = 4
+Y = 4
+CORES = 2
+GROUP = Y * CORES
+OWN = 16
+
+
+def exchange_kernel(
+    heads,
+    slot_prompt_ref,
+    query_ref,
+    own_ref,
+    cache_ref,
+    out_ref,
+    sent,
+    held,
+    done,
+    back,
+    slot_of,
+    sent_sem,
+    held_sem,
+    done_sem,
+    back_sem,
+):
+    prompts, query_rows, head_size = query_ref.shape
+    width = sent.shape[1]
+    here = lax.axis_index("samp")
+    here_z = here // GROUP
+    here_y = lax.rem(here, GROUP) // CORES
+    here_core = lax.rem(here, CORES)
+
+    def z_distance(group):
+        return lax.rem(group * (group + 1) // 2, Z_HI)
+
+    def partner(group, member, away):
+        dz = z_distance(group)
+        dy = member // CORES
+        dcore = lax.rem(member, CORES)
+        if not away:
+            dz = Z_HI - dz
+            dy = Y - dy
+        z = lax.rem(here_z + dz, Z_HI)
+        y = lax.rem(here_y + dy, Y)
+        core = lax.rem(here_core + dcore, CORES)
+        return z * GROUP + y * CORES + core
+
+    def remote(src, dst, send, recv, device):
+        return pltpu.make_async_remote_copy(
+            src_ref=src,
+            dst_ref=dst,
+            send_sem=send,
+            recv_sem=recv,
+            device_id={"samp": device},
+            device_id_type=pl.DeviceIdType.MESH,
+        )
+
+    def fill(group, member, into):
+        slot = partner(group, member, True)
+        prompt = slot_prompt_ref[slot]
+        at = group * GROUP + member
+        into[at, :query_rows] = query_ref[prompt]
+        own = own_ref[prompt]
+        into[at, query_rows : query_rows + OWN] = own[:, :head_size]
+        into[at, query_rows + OWN :] = own[:, head_size:]
+
+    barrier = pltpu.get_barrier_semaphore()
+
+    def greet(at, carry):
+        pl.semaphore_signal(
+            barrier,
+            inc=1,
+            device_id={"samp": partner(at // GROUP, lax.rem(at, GROUP), True)},
+            device_id_type=pl.DeviceIdType.MESH,
+        )
+        return carry
+
+    lax.fori_loop(1, prompts, greet, 0)
+    fill(0, 0, held)
+
+    def prepare(at, carry):
+        fill(at // GROUP, lax.rem(at, GROUP), sent)
+        return carry
+
+    lax.fori_loop(1, prompts, prepare, 0)
+
+    def send_out(at, carry):
+        group = at // GROUP
+        remote(
+            sent.at[at],
+            held.at[at],
+            sent_sem,
+            held_sem.at[group],
+            partner(group, lax.rem(at, GROUP), True),
+        ).start()
+        return carry
+
+    pl.semaphore_wait(barrier, prompts - 1)
+    for group in range(Z_HI - 1, -1, -1):
+        lax.fori_loop(max(1, group * GROUP), (group + 1) * GROUP, send_out, 0)
+
+    def find(prompt, carry):
+        def look(slot, found):
+            return jnp.where(slot_prompt_ref[slot] == prompt, slot, found)
+
+        slot_of[prompt] = lax.fori_loop(0, prompts, look, 0)
+        return carry
+
+    lax.fori_loop(0, prompts, find, 0)
+
     factor = math.log2(math.e) / math.sqrt(head_size)
     nt = (((1,), (1,)), ((), ()))
     nn = (((1,), (0,)), ((), ()))
-    query = sent_ref[:, :query_rows, :].reshape(sources * query_rows, head_size)
-    own = sent_ref[:, query_rows:, :].astype(jnp.float32)
-    own = own.reshape(sources * own_rows, head_size).astype(jnp.bfloat16)
-    total_own = sources * own_rows
-    at = lax.broadcasted_iota(jnp.int32, (total_own, total_own), 0)
-    taken = lax.broadcasted_iota(jnp.int32, (total_own, total_own), 1)
-    move = jnp.where((taken == at + 1) & (lax.rem(at, 2) == 0), 1.0, 0.0).astype(jnp.bfloat16)
-    own_value = lax.dot_general(move, own, nn, preferred_element_type=jnp.float32)
-    own_value = own_value.astype(jnp.bfloat16)
-    prompt_score = lax.dot_general(
-        query, cache_ref[:, :head_size], nt, preferred_element_type=jnp.float32
-    )
-    own_score = lax.dot_general(query, own, nt, preferred_element_type=jnp.float32)
-    row = lax.broadcasted_iota(jnp.int32, own_score.shape, 0) // group_size
-    column = lax.broadcasted_iota(jnp.int32, own_score.shape, 1)
-    key = column // 2
-    seen = (lax.rem(column, 2) == 0) & (key <= row) & (key >= row - lax.rem(row, STEPS))
-    own_score = jnp.where(seen, own_score, -jnp.inf)
-    maximum = jnp.maximum(
-        jnp.max(prompt_score, -1, keepdims=True), jnp.max(own_score, -1, keepdims=True)
-    )
-    shift = maximum * factor
-    prompt_weight = jnp.exp2(prompt_score * factor - shift)
-    own_weight = jnp.exp2(own_score * factor - shift)
-    denominator = jnp.sum(prompt_weight, -1, keepdims=True) + jnp.sum(
-        own_weight, -1, keepdims=True
-    )
-    summed = lax.dot_general(
-        prompt_weight.astype(jnp.bfloat16),
-        cache_ref[:, head_size:],
-        nn,
-        preferred_element_type=jnp.float32,
-    )
-    summed = summed + lax.dot_general(
-        own_weight.astype(jnp.bfloat16), own_value, nn, preferred_element_type=jnp.float32
-    )
-    attended = (summed / denominator).astype(jnp.bfloat16)
-    out_ref[...] = attended.reshape(sources, query_rows, head_size)
-
-
-def attend(sent, cache, query_rows, group_size):
-    sources, width, head_size = sent.shape
-    block = min(SOURCES_PER_BLOCK, sources)
+
+    def attend(group, first):
+        base = group * GROUP
+        count = GROUP - 1 if first else GROUP
+        start = base + GROUP - count
+        arrived = held.at[pl.ds(start, count)]
+        pltpu.make_async_copy(arrived, arrived, held_sem.at[group]).wait()
+        query = held[pl.ds(base, GROUP), :query_rows].reshape(GROUP * query_rows, head_size)
+        key = held[pl.ds(base, GROUP), query_rows : query_rows + OWN]
+        key = key.reshape(GROUP * OWN, head_size)
+        value = held[pl.ds(base, GROUP), query_rows + OWN :].reshape(GROUP * OWN, head_size)
+        prompt_score = lax.dot_general(
+            query, cache_ref[:, :head_size], nt, preferred_element_type=jnp.float32
+        )
+        own_score = lax.dot_general(query, key, nt, preferred_element_type=jnp.float32)
+        line = lax.broadcasted_iota(jnp.int32, own_score.shape, 0)
+        column = lax.broadcasted_iota(jnp.int32, own_score.shape, 1)
+        row = lax.rem(line, query_rows) // heads
+        own = lax.rem(column, OWN)
+        seen = (line // query_rows == column // OWN) & (own <= row)
+        seen = seen & (own >= row - lax.rem(row, STEPS))
+        own_score = jnp.where(seen, own_score, -jnp.inf)
+        maximum = jnp.maximum(
+            jnp.max(prompt_score, -1, keepdims=True), jnp.max(own_score, -1, keepdims=True)
+        )
+        shift = maximum * factor
+        prompt_weight = jnp.exp2(prompt_score * factor - shift)
+        own_weight = jnp.exp2(own_score * factor - shift)
+        denominator = jnp.sum(prompt_weight, -1, keepdims=True) + jnp.sum(
+            own_weight, -1, keepdims=True
+        )
+        summed = lax.dot_general(
+            prompt_weight.astype(jnp.bfloat16),
+            cache_ref[:, head_size:],
+            nn,
+            preferred_element_type=jnp.float32,
+        )
+        summed = summed + lax.dot_general(
+            own_weight.astype(jnp.bfloat16), value, nn, preferred_element_type=jnp.float32
+        )
+        attended = (summed / denominator).astype(jnp.bfloat16)
+        attended = attended.reshape(GROUP, query_rows, head_size)
+        done[pl.ds(base, GROUP)] = attended
+        if first:
+            back[0] = attended[0]
+
+        def send_back(at, carry):
+            remote(
+                done.at[at],
+                back.at[at],
+                done_sem,
+                back_sem,
+                partner(group, at - base, False),
+            ).start()
+            return carry
+
+        lax.fori_loop(start, base + GROUP, send_back, 0)
+
+    attend(0, True)
+
+    def attend_next(group, carry):
+        attend(group, False)
+        return carry
+
+    lax.fori_loop(1, Z_HI, attend_next, 0)
+    others = sent.at[pl.ds(1, prompts - 1)]
+    pltpu.make_async_copy(others, others, sent_sem).wait()
+    others = done.at[pl.ds(1, prompts - 1)]
+    pltpu.make_async_copy(others, others, done_sem).wait()
+    others = back.at[pl.ds(1, prompts - 1)]
+    pltpu.make_async_copy(others, others, back_sem).wait()
+
+    def place(prompt, carry):
+        slot = slot_of[prompt]
+        dz = lax.rem(slot // GROUP - here_z + Z_HI, Z_HI)
+        dy = lax.rem(lax.rem(slot, GROUP) // CORES - here_y + Y, Y)
+        dcore = lax.rem(lax.rem(slot, CORES) + here_core, CORES)
+        out_ref[prompt] = back[z_distance(dz) * GROUP + dy * CORES + dcore]
+        return carry
+
+    lax.fori_loop(0, prompts, place, 0)
+
+
+def exchange(slot_prompt, query, own, cache, heads):
+    prompts, query_rows, head_size = query.shape
+    width = query_rows + 2 * OWN
+    held = jnp.bfloat16
+    dma = pltpu.SemaphoreType.DMA
+    vmem = pl.BlockSpec(memory_space=pltpu.VMEM)
     return pl.pallas_call(
-        lambda *refs: attend_kernel(group_size, *refs),
-        grid=(sources // block,),
-        in_specs=[
-            pl.BlockSpec((block, width, head_size), lambda i: (i, 0, 0)),
-            pl.BlockSpec(cache.shape, lambda i: (0, 0)),
+        functools.partial(exchange_kernel, heads),
+        in_specs=[pl.BlockSpec(memory_space=pltpu.SMEM), vmem, vmem, vmem],
+        out_specs=vmem,
+        out_shape=jax.ShapeDtypeStruct(query.shape, held),
+        scratch_shapes=[
+            pltpu.VMEM((prompts, width, head_size), held),
+            pltpu.VMEM((prompts, width, head_size), held),
+            pltpu.VMEM(query.shape, held),
+            pltpu.VMEM(query.shape, held),
+            pltpu.SMEM((prompts,), jnp.int32),
+            dma,
+            dma((Z_HI,)),
+            dma,
+            dma,
         ],
-        out_specs=pl.BlockSpec((block, query_rows, head_size), lambda i: (i, 0, 0)),
-        out_shape=jax.ShapeDtypeStruct((sources, query_rows, head_size), jnp.bfloat16),
-        compiler_params=pltpu.CompilerParams(vmem_limit_bytes=40 * 2**20),
-    )(sent, cache)
+        compiler_params=pltpu.CompilerParams(
+            collective_id=1, has_side_effects=True, vmem_limit_bytes=40 * 2**20
+        ),
+    )(slot_prompt, query, own, cache)
 
 
 RING = 4
@@ -332,22 +490,17 @@
 
 def on_device(queries, cache, new_kv, slot_prompt, residual, out_weight, gain):
     row_total, heads_local, head_size = queries.shape
-    group_size = heads_local // new_kv.shape[1]
-    prompt_count = slot_prompt.shape[0]
-    rows = row_total // prompt_count
-    packed = jnp.concatenate(
-        [
-            queries.reshape(prompt_count, rows * heads_local, head_size),
-            new_kv.reshape(prompt_count, rows * 2, head_size),
-        ],
-        axis=1,
+    prompts = slot_prompt.shape[0]
+    rows = row_total // prompts
+    own = jnp.pad(new_kv.reshape(prompts, rows, 2 * head_size), ((0, 0), (0, OWN - rows), (0, 0)))
+    attended = exchange(
+        slot_prompt,
+        queries.reshape(prompts, rows * heads_local, head_size),
+        own,
+        cache.reshape(cache.shape[1], 2 * head_size),
+        heads_local,
     )
-    sent = jnp.take(packed, slot_prompt, axis=0)
-    sent = lax.all_to_all(sent, "samp", 0, 0, tiled=True)
-    attended = attend(sent, cache.reshape(cache.shape[1], 2 * head_size), rows * heads_local, group_size)
-    attended = lax.all_to_all(attended, "samp", 0, 0, tiled=True)
-    slot_of = jnp.zeros_like(slot_prompt).at[slot_prompt].set(jnp.arange(prompt_count, dtype=jnp.int32))
-    attended = jnp.take(attended, slot_of, axis=0).reshape(row_total, heads_local * head_size)
+    attended = attended.reshape(row_total, heads_local * head_size)
     projected = project(attended, out_weight).astype(jnp.float32)
     hidden = (residual.astype(jnp.float32) + projected).astype(jnp.bfloat16)
     hidden_f = hidden.astype(jnp.float32)

time: 123 us -> 109 us (0.89)
  Pallas kernels: 60.7 us -> 100 us
  blocking collectives: 31.7 us -> 0 us
  waiting for transfers between devices: 15 us -> 0 us
  starting transfers between devices: 4.89 us -> 0 us
  other arithmetic: 4.14 us -> 1.52 us
    pallas_call x1, Pallas kernels: 6.32 us -> 46.2 us  [exchange(): pl.pallas_call(functools.partial(exchange_kernel, heads), in_specs=[pl.Bl...]
    all_to_all x1 -> x0, blocking collectives: 31.7 us -> none  [on_device(): sent = lax.all_to_all(sent, 'samp', 0, 0, tiled=True)]
    all_to_all x1 -> x0, waiting for transfers between devices: 15 us -> none  [on_device(): attended = lax.all_to_all(attended, 'samp', 0, 0, tiled=True)]
    all_to_all x1 -> x0, starting transfers between devices: 4.89 us -> none  [on_device(): attended = lax.all_to_all(attended, 'samp', 0, 0, tiled=True)]
    unnamed x8 -> x12, local copies, waits for them, and re-layouts: 0.36 us -> 3.04 us
    gather x2 -> x0, local copies, waits for them, and re-layouts: 1.29 us -> none  [the longest x1 0.67 us: on_device(): sent = jnp.take(packed, slot_prompt, axis=0)]
  transfers between devices with their start and end apart: 1 -> 0, of which waited for: 1 -> 0; matrix products, arithmetic and copies ran while one was open for 1% -> 0% of each run, Pallas kernels for 0% -> 0%
where the time goes in v3:
time: 109 us; the launch traced here: 107 us
  Pallas kernels  100 us (92%)
  local copies, waits for them, and re-layouts  4.28 us (4%)
  other arithmetic  1.52 us (1%)
    pallas_call x1, Pallas kernels, project(): pl.pallas_call(project_kernel, in_specs=[pl.BlockSpec(memory_space=pltpu....  54.3 us
    pallas_call x1, Pallas kernels, exchange(): pl.pallas_call(functools.partial(exchange_kernel, heads), in_specs=[pl.Bl...  46.2 us
    unnamed x12, local copies, waits for them, and re-layouts  3.04 us

profile of v3, /device:TPU:1, one launch (start us, length us, event | category | flops | bytes accessed | tf_op | source)
XLA Modules:
  0.0 106.9 jit_solution(16001252145582132199)
XLA Ops:
  0.6 1.0 reshape.23
  1.6 0.0 copy-start
  1.7 1.0 copy-done
  2.7 0.0 copy-start.1
  2.7 1.0 copy-done.1
  3.7 0.0 copy-start.2
  3.7 0.7 copy-done.2
  4.3 46.2 %shard_map.86 = bf16[32,48,128]{2,1,0:T(8,128)(2,1)S(1)} custom-call(s32[32]{0:T(128)S(1)} %copy-done.2, bf16[32,48,128]{2,1,0:T(8,128)(2,1)S(1)} %bitcast.5, bf16[32,16,256]{2,1,0:T(8,128)(2,1)S(1)} %pad.4.own_ref, bf16[1024,256]{1,0:T(8,128)(2,1)S(1)} %bitcast.4), custom_call_target="tpu_custom_call" | custom-call | tf_op jit(solution)/shard_map/pallas_call | solution.py:213
  50.5 0.2 reshape.25.attended_ref
  50.8 0.0 copy-start.4
  50.8 54.3 %shard_map.87 = bf16[48,8192]{1,0:T(8,128)(2,1)S(1)} custom-call(bf16[384,512]{1,0:T(8,128)(2,1)S(1)} %reshape.25.attended_ref, bf16[512,8192]{1,0:T(8,128)(2,1)} %weight_hbm.1), custom_call_target="tpu_custom_call" | custom-call | flops 3221225472 | bytes 9568256 | tf_op jit(solution)/shard_map/pallas_call | solution.py:454
  105.0 0.0 copy-done.4
  105.1 0.0 copy-start.5
  105.1 0.4 fusion
  105.4 0.0 copy-start.3
  105.5 0.3 copy-done.5
  105.8 1.1 %fusion.2 = bf16[48,8192]{1,0:T(8,128)(2,1)} fusion(bf16[48,8192]{1,0:T(8,128)(2,1)S(1)} %get-tuple-element.3, f32[8192]{0:T(1024)S(1)} %copy-done.5, f32[48]{0:T(128)S(1)} %add_sqrt_fusion), kind=kLoop, calls=%fused_computation.4 | loop fusion | flops 1572864 | bytes 1605824 | tf_op jit(solution)/shard_map/convert_element_type | solution.py:508
  106.9 0.0 copy-done.3
  (2 shorter events, 0.0 us)
Async XLA Ops:
  1.6 1.0 copy-start
  2.7 1.0 copy-start.1
  3.7 0.7 copy-start.2
  50.8 54.3 %copy-start.4 = (bf16[48,8192]{1,0:T(8,128)(2,1)S(1)}, bf16[48,8192]{1,0:T(8,128)(2,1)}, u32[]{:S(2)}) copy-start(bf16[48,8192]{1,0:T(8,128)(2,1)} %param.11) | copy-start | bytes 2359300
  105.1 0.8 copy-start.5
  105.4 1.5 %copy-start.3 = (bf16[48,8192]{1,0:T(8,128)(2,1)}, bf16[48,8192]{1,0:T(8,128)(2,1)S(1)}, u32[]{:S(2)}) copy-start(bf16[48,8192]{1,0:T(8,128)(2,1)S(1)} %get-tuple-element.3) | copy-start | bytes 2359300

commit v4 on v3

--- a/solution.py
+++ b/solution.py
@@ -19,15 +19,20 @@
 def exchange_kernel(
     heads,
     slot_prompt_ref,
+    query_hbm,
+    own_hbm,
+    cache_hbm,
+    out_ref,
     query_ref,
     own_ref,
+    own_rows,
     cache_ref,
-    out_ref,
     sent,
     held,
     done,
     back,
     slot_of,
+    load_sem,
     sent_sem,
     held_sem,
     done_sem,
@@ -74,6 +79,13 @@
         into[at, query_rows : query_rows + OWN] = own[:, :head_size]
         into[at, query_rows + OWN :] = own[:, head_size:]
 
+    loads = [
+        pltpu.make_async_copy(query_hbm, query_ref, load_sem.at[0]),
+        pltpu.make_async_copy(own_hbm, own_rows, load_sem.at[1]),
+        pltpu.make_async_copy(cache_hbm, cache_ref, load_sem.at[2]),
+    ]
+    for load in loads:
+        load.start()
     barrier = pltpu.get_barrier_semaphore()
 
     def greet(at, carry):
@@ -86,6 +98,16 @@
         return carry
 
     lax.fori_loop(1, prompts, greet, 0)
+    loads[1].wait()
+    rows = own_rows.shape[0] // prompts
+    together = OWN // math.gcd(OWN, rows)
+    blank = jnp.zeros((OWN - rows, own_ref.shape[2]), jnp.float32)
+    for first in range(0, prompts, together):
+        block = own_rows[first * rows : (first + together) * rows].astype(jnp.float32)
+        for prompt in range(together):
+            piece = jnp.concatenate([block[prompt * rows : (prompt + 1) * rows], blank], axis=0)
+            own_ref[first + prompt] = piece.astype(jnp.bfloat16)
+    loads[0].wait()
     fill(0, 0, held)
 
     def prepare(at, carry):
@@ -106,7 +128,7 @@
         return carry
 
     pl.semaphore_wait(barrier, prompts - 1)
-    for group in range(Z_HI - 1, -1, -1):
+    for group in range(Z_HI):
         lax.fori_loop(max(1, group * GROUP), (group + 1) * GROUP, send_out, 0)
 
     def find(prompt, carry):
@@ -179,6 +201,7 @@
 
         lax.fori_loop(start, base + GROUP, send_back, 0)
 
+    loads[2].wait()
     attend(0, True)
 
     def attend_next(group, carry):
@@ -204,37 +227,92 @@
     lax.fori_loop(0, prompts, place, 0)
 
 
-def exchange(slot_prompt, query, own, cache, heads):
+def exchange(slot_prompt, query, own_rows, cache, heads):
     prompts, query_rows, head_size = query.shape
     width = query_rows + 2 * OWN
     held = jnp.bfloat16
     dma = pltpu.SemaphoreType.DMA
-    vmem = pl.BlockSpec(memory_space=pltpu.VMEM)
+    hbm = pl.BlockSpec(memory_space=pl.ANY)
     return pl.pallas_call(
         functools.partial(exchange_kernel, heads),
-        in_specs=[pl.BlockSpec(memory_space=pltpu.SMEM), vmem, vmem, vmem],
-        out_specs=vmem,
+        in_specs=[pl.BlockSpec(memory_space=pltpu.SMEM), hbm, hbm, hbm],
+        out_specs=pl.BlockSpec(memory_space=pltpu.VMEM),
         out_shape=jax.ShapeDtypeStruct(query.shape, held),
         scratch_shapes=[
+            pltpu.VMEM(query.shape, held),
+            pltpu.VMEM((prompts, OWN, 2 * head_size), held),
+            pltpu.VMEM(own_rows.shape, held),
+            pltpu.VMEM(cache.shape, held),
             pltpu.VMEM((prompts, width, head_size), held),
             pltpu.VMEM((prompts, width, head_size), held),
             pltpu.VMEM(query.shape, held),
             pltpu.VMEM(query.shape, held),
             pltpu.SMEM((prompts,), jnp.int32),
+            dma((3,)),
             dma,
             dma((Z_HI,)),
             dma,
             dma,
         ],
         compiler_params=pltpu.CompilerParams(
-            collective_id=1, has_side_effects=True, vmem_limit_bytes=40 * 2**20
+            collective_id=1, has_side_effects=True, vmem_limit_bytes=60 * 2**20
         ),
-    )(slot_prompt, query, own, cache)
+    )(slot_prompt, query, own_rows, cache)
 
 
 RING = 4
-RING_FIRST = 5
-PAIR_FIRST = 3
+RING_UNITS = (2, 2, 2, 2, 1)
+PAIR_UNITS = (2, 2, 2, 1)
+RING_FIRST = len(RING_UNITS)
+PAIR_FIRST = len(PAIR_UNITS)
+START_RING, START_PAIR, RING_STEP, RING_END, PAIR_STEP, PAIR_RING = range(6)
+ORDER = (
+    (START_RING, 4, 0),
+    (START_PAIR, 3, 0),
+    (START_RING, 2, 0),
+    (START_RING, 1, 0),
+    (RING_STEP, 4, 0),
+    (START_PAIR, 2, 0),
+    (PAIR_STEP, 3, 0),
+    (START_RING, 0, 0),
+    (RING_STEP, 4, 1),
+    (START_PAIR, 1, 0),
+    (RING_STEP, 1, 0),
+    (START_PAIR, 0, 0),
+    (PAIR_RING, 3, 0),
+    (START_RING, 3, 0),
+    (PAIR_STEP, 2, 0),
+    (RING_STEP, 0, 0),
+    (RING_STEP, 4, 2),
+    (RING_STEP, 2, 0),
+    (RING_STEP, 1, 1),
+    (PAIR_RING, 3, 1),
+    (RING_STEP, 3, 0),
+    (RING_STEP, 0, 1),
+    (PAIR_RING, 2, 0),
+    (PAIR_STEP, 1, 0),
+    (RING_STEP, 2, 1),
+    (RING_STEP, 1, 2),
+    (PAIR_RING, 3, 2),
+    (RING_STEP, 3, 1),
+    (RING_STEP, 0, 2),
+    (PAIR_STEP, 0, 0),
+    (PAIR_RING, 2, 1),
+    (PAIR_RING, 1, 0),
+    (RING_STEP, 2, 2),
+    (RING_END, 4, 0),
+    (RING_END, 1, 0),
+    (RING_STEP, 3, 2),
+    (RING_END, 0, 0),
+    (PAIR_RING, 0, 0),
+    (PAIR_RING, 2, 2),
+    (PAIR_RING, 1, 1),
+    (RING_END, 2, 0),
+    (PAIR_RING, 0, 1),
+    (RING_END, 3, 0),
+    (PAIR_RING, 1, 2),
+    (PAIR_RING, 0, 2),
+)
 
 
 def project_kernel(
@@ -259,8 +337,6 @@
     zr_recv,
 ):
     rows = out_ref.shape[0]
-    width = weight.shape[2]
-    chunks = weight.shape[0]
     here = lax.axis_index("tp")
     x = lax.rem(here, RING)
     z = here // RING
@@ -276,15 +352,27 @@
         ahead = 2 * RING - 1 - step if way == 0 else 1 + step
         return lax.rem(x + ahead, RING)
 
-    def ring_chunk(k, way):
-        return 2 * k + way
-
-    def pair_chunk(k, way):
-        return 2 * RING_FIRST + 2 * k + way
+    unit = out_ref.shape[1] // (2 * (sum(RING_UNITS) + sum(PAIR_UNITS)))
+    chunks = {}
+    start = 0
+    for units in (RING_UNITS, PAIR_UNITS):
+        for k in range(len(units)):
+            for way in range(2):
+                chunks[(units is RING_UNITS, k, way)] = (len(chunks), start, units[k] * unit)
+                start += units[k] * unit
+
+    def ring_width(k):
+        return RING_UNITS[k] * unit
+
+    def pair_width(k):
+        return PAIR_UNITS[k] * unit
 
     def fetch(chunk):
+        index, start, width = chunk
         return pltpu.make_async_copy(
-            weight_hbm.at[:, pl.ds(chunk * width, width)], weight.at[chunk], weight_sem.at[chunk]
+            weight_hbm.at[:, pl.ds(start, width)],
+            weight.at[index, :, pl.ds(0, width)],
+            weight_sem.at[index],
         )
 
     def remote(src, dst, send, recv, device):
@@ -299,8 +387,8 @@
 
     def ring_copy(k, way, step):
         return remote(
-            xp.at[way, k, block(way, step)],
-            xr.at[way, k, step],
+            xp.at[way, k, block(way, step), :, :, pl.ds(0, ring_width(k))],
+            xr.at[way, k, step, :, :, pl.ds(0, ring_width(k))],
             xr_send.at[way, k, step],
             xr_recv.at[way, k, step],
             ring_device(way),
@@ -308,8 +396,8 @@
 
     def ring_pair_copy(k, way):
         return remote(
-            xp.at[way, k, x, other],
-            xq.at[way, k],
+            xp.at[way, k, x, other, :, pl.ds(0, ring_width(k))],
+            xq.at[way, k, :, pl.ds(0, ring_width(k))],
             xq_send.at[way, k],
             xq_recv.at[way, k],
             pair_device,
@@ -317,8 +405,8 @@
 
     def pair_copy(k, way):
         return remote(
-            zp.at[way, k, other],
-            zq.at[way, k],
+            zp.at[way, k, other, :, :, pl.ds(0, pair_width(k))],
+            zq.at[way, k, :, :, pl.ds(0, pair_width(k))],
             zq_send.at[way, k],
             zq_recv.at[way, k],
             pair_device,
@@ -326,8 +414,8 @@
 
     def pair_ring_copy(k, way, step):
         return remote(
-            zp.at[way, k, z, block(way, step)],
-            zr.at[way, k, step],
+            zp.at[way, k, z, block(way, step), :, pl.ds(0, pair_width(k))],
+            zr.at[way, k, step, :, pl.ds(0, pair_width(k))],
             zr_send.at[way, k, step],
             zr_recv.at[way, k, step],
             ring_device(way),
@@ -335,71 +423,76 @@
 
     def multiply(chunk):
         fetch(chunk).wait()
+        index, _, width = chunk
         product = jnp.dot(
-            attended_ref[...], weight[chunk], preferred_element_type=jnp.float32
+            attended_ref[...], weight[index, :, :width], preferred_element_type=jnp.float32
         )
         return product.astype(jnp.bfloat16)
 
-    def start_ring(k):
-        for way in range(2):
-            product = multiply(ring_chunk(k, way))
-            for j in range(2 * RING):
-                xp[way, k, j % RING, j // RING] = product[j * rows : (j + 1) * rows]
-            ring_copy(k, way, 0).start()
-
-    def start_pair(k):
-        for way in range(2):
-            product = multiply(pair_chunk(k, way))
-            for j in range(2 * RING):
-                zp[way, k, j // RING, j % RING] = product[j * rows : (j + 1) * rows]
-            pair_copy(k, way).start()
+    def start_ring(k, way):
+        product = multiply(chunks[(True, k, way)])
+        for j in range(2 * RING):
+            part = product[j * rows : (j + 1) * rows]
+            xp[way, k, j % RING, j // RING, :, : ring_width(k)] = part
+        ring_copy(k, way, 0).start()
+
+    def start_pair(k, way):
+        product = multiply(chunks[(False, k, way)])
+        for j in range(2 * RING):
+            part = product[j * rows : (j + 1) * rows]
+            zp[way, k, j // RING, j % RING, :, : pair_width(k)] = part
+        pair_copy(k, way).start()
 
     def wide(value):
         return value.astype(jnp.float32)
 
-    def ring_step(k, step):
-        for way in range(2):
-            ring_copy(k, way, step).wait_recv()
-            at = block(way, step + 1)
-            xp[way, k, at] = (wide(xp[way, k, at]) + wide(xr[way, k, step])).astype(jnp.bfloat16)
-            if step < RING - 2:
-                ring_copy(k, way, step + 1).start()
-            else:
-                ring_pair_copy(k, way).start()
-
-    def ring_end(k):
-        for way in range(2):
-            ring_pair_copy(k, way).wait_recv()
-            columns = pl.ds(ring_chunk(k, way) * width, width)
-            out_ref[:, columns] = (wide(xp[way, k, x, z]) + wide(xq[way, k])).astype(jnp.bfloat16)
-
-    def pair_step(k):
-        for way in range(2):
-            pair_copy(k, way).wait_recv()
-            at = block(way, 0)
-            zp[way, k, z, at] = (wide(zp[way, k, z, at]) + wide(zq[way, k, at])).astype(
-                jnp.bfloat16
-            )
-            pair_ring_copy(k, way, 0).start()
-
-    def pair_ring_step(k, step):
-        for way in range(2):
-            pair_ring_copy(k, way, step).wait_recv()
-            at = block(way, step + 1)
-            total = wide(zp[way, k, z, at]) + wide(zq[way, k, at]) + wide(zr[way, k, step])
-            if step < RING - 2:
-                zp[way, k, z, at] = total.astype(jnp.bfloat16)
-                pair_ring_copy(k, way, step + 1).start()
-            else:
-                columns = pl.ds(pair_chunk(k, way) * width, width)
-                out_ref[:, columns] = total.astype(jnp.bfloat16)
-
-    order = []
-    for k in range(max(RING_FIRST, PAIR_FIRST)):
-        order += [pair_chunk(k, way) for way in range(2)] if k < PAIR_FIRST else []
-        order += [ring_chunk(k, way) for way in range(2)] if k < RING_FIRST else []
-    for chunk in order:
-        fetch(chunk).start()
+    def finish(chunk, total):
+        _, start, width = chunk
+        out_ref[:, start : start + width] = total.astype(jnp.bfloat16)
+
+    def ring_step(k, way, step):
+        ring_copy(k, way, step).wait_recv()
+        at = block(way, step + 1)
+        width = ring_width(k)
+        total = wide(xp[way, k, at, :, :, :width]) + wide(xr[way, k, step, :, :, :width])
+        xp[way, k, at, :, :, :width] = total.astype(jnp.bfloat16)
+        if step < RING - 2:
+            ring_copy(k, way, step + 1).start()
+        else:
+            ring_pair_copy(k, way).start()
+
+    def ring_end(k, way):
+        ring_pair_copy(k, way).wait_recv()
+        width = ring_width(k)
+        finish(
+            chunks[(True, k, way)],
+            wide(xp[way, k, x, z, :, :width]) + wide(xq[way, k, :, :width]),
+        )
+
+    def pair_step(k, way):
+        pair_copy(k, way).wait_recv()
+        at = block(way, 0)
+        width = pair_width(k)
+        total = wide(zp[way, k, z, at, :, :width]) + wide(zq[way, k, at, :, :width])
+        zp[way, k, z, at, :, :width] = total.astype(jnp.bfloat16)
+        pair_ring_copy(k, way, 0).start()
+
+    def pair_ring_step(k, way, step):
+        pair_ring_copy(k, way, step).wait_recv()
+        at = block(way, step + 1)
+        width = pair_width(k)
+        total = wide(zp[way, k, z, at, :, :width]) + wide(zq[way, k, at, :, :width])
+        total = total + wide(zr[way, k, step, :, :width])
+        if step < RING - 2:
+            zp[way, k, z, at, :, :width] = total.astype(jnp.bfloat16)
+            pair_ring_copy(k, way, step + 1).start()
+        else:
+            finish(chunks[(False, k, way)], total)
+
+    for kind, k, _ in ORDER:
+        if kind in (START_RING, START_PAIR):
+            for way in range(2):
+                fetch(chunks[(kind == START_RING, k, way)]).start()
     barrier = pltpu.get_barrier_semaphore()
     for device in (ring_device(0), ring_device(1), pair_device):
         pl.semaphore_signal(
@@ -407,30 +500,20 @@
         )
     pl.semaphore_wait(barrier, 3)
 
-    for k in range(max(RING_FIRST, PAIR_FIRST)):
-        if k < PAIR_FIRST:
-            start_pair(k)
-        if k < RING_FIRST:
-            start_ring(k)
-    steps = []
-    for k in range(RING_FIRST):
-        for step in range(RING - 1):
-            steps.append((step + (k + 1) / RING_FIRST, 0, k, step))
-        steps.append((3.2 + (k + 1) * 1.0 / RING_FIRST, 1, k, 0))
-    for k in range(PAIR_FIRST):
-        arrival = 3.0 * (k + 1) / PAIR_FIRST
-        steps.append((arrival, 2, k, 0))
-        for step in range(RING - 1):
-            steps.append((arrival + 0.45 * (step + 1), 3, k, step))
-    for _, kind, k, step in sorted(steps):
-        if kind == 0:
-            ring_step(k, step)
-        elif kind == 1:
-            ring_end(k)
-        elif kind == 2:
-            pair_step(k)
-        else:
-            pair_ring_step(k, step)
+    for kind, k, step in ORDER:
+        for way in range(2):
+            if kind == START_RING:
+                start_ring(k, way)
+            elif kind == START_PAIR:
+                start_pair(k, way)
+            elif kind == RING_STEP:
+                ring_step(k, way, step)
+            elif kind == RING_END:
+                ring_end(k, way)
+            elif kind == PAIR_STEP:
+                pair_step(k, way)
+            else:
+                pair_ring_step(k, way, step)
     for way in range(2):
         for k in range(RING_FIRST):
             for step in range(RING - 1):
@@ -447,7 +530,8 @@
     columns = out_weight.shape[1]
     rows = total // (2 * RING)
     chunks = 2 * (RING_FIRST + PAIR_FIRST)
-    width = columns // chunks
+    units = 2 * (sum(RING_UNITS) + sum(PAIR_UNITS))
+    width = max(RING_UNITS + PAIR_UNITS) * columns // units
     steps = RING - 1
     dma = pltpu.SemaphoreType.DMA
     held = jnp.bfloat16
@@ -492,11 +576,10 @@
     row_total, heads_local, head_size = queries.shape
     prompts = slot_prompt.shape[0]
     rows = row_total // prompts
-    own = jnp.pad(new_kv.reshape(prompts, rows, 2 * head_size), ((0, 0), (0, OWN - rows), (0, 0)))
     attended = exchange(
         slot_prompt,
         queries.reshape(prompts, rows * heads_local, head_size),
-        own,
+        new_kv.reshape(row_total, 2 * head_size),
         cache.reshape(cache.shape[1], 2 * head_size),
         heads_local,
     )

time: 109 us -> 95.6 us (0.88)
  Pallas kernels: 100 us -> 90.4 us
  local copies, waits for them, and re-layouts: 4.28 us -> 1.59 us
    pallas_call x1, Pallas kernels: 54.3 us -> 47.1 us  [project(): pl.pallas_call(project_kernel, in_specs=[pl.BlockSpec(memory_space=pltpu....]
    pallas_call x1, Pallas kernels: 46.2 us -> 43.3 us  [exchange(): pl.pallas_call(functools.partial(exchange_kernel, heads), in_specs=[pl.Bl...]
    unnamed x12 -> x6, local copies, waits for them, and re-layouts: 3.04 us -> 0.36 us
where the time goes in v4:
time: 95.6 us; the launch traced here: 94.2 us
  Pallas kernels  90.4 us (95%)
  local copies, waits for them, and re-layouts  1.59 us (2%)
  other arithmetic  1.52 us (2%)
    pallas_call x1, Pallas kernels, project(): pl.pallas_call(project_kernel, in_specs=[pl.BlockSpec(memory_space=pltpu....  47.1 us
    pallas_call x1, Pallas kernels, exchange(): pl.pallas_call(functools.partial(exchange_kernel, heads), in_specs=[pl.Bl...  43.3 us

profile of v4, /device:TPU:1, one launch (start us, length us, event | category | flops | bytes accessed | tf_op | source)
XLA Modules:
  0.0 94.2 jit_solution(4815126709338288317)
XLA Ops:
  0.6 43.3 %shard_map.86 = bf16[32,48,128]{2,1,0:T(8,128)(2,1)} custom-call(s32[32]{0:T(128)} %slot_prompt_ref.1, bf16[32,48,128]{2,1,0:T(8,128)(2,1)} %bitcast.4, bf16[384,256]{1,0:T(8,128)(2,1)} %bitcast.5, bf16[1024,256]{1,0:T(8,128)(2,1)} %bitcast.3), custom_call_target="tpu_custom_call" | custom-call | tf_op jit(solution)/shard_map/pallas_call | solution.py:236
  43.9 1.2 %reshape.25.attended_ref = bf16[384,512]{1,0:T(8,128)(2,1)S(1)} reshape(bf16[32,48,128]{2,1,0:T(8,128)(2,1)} %shard_map.86) | data formatting | bytes 786432 | tf_op jit(solution)/shard_map/reshape | solution.py:586
  45.1 0.0 copy-start.1
  45.1 47.1 %shard_map.87 = bf16[48,8192]{1,0:T(8,128)(2,1)S(1)} custom-call(bf16[384,512]{1,0:T(8,128)(2,1)S(1)} %reshape.25.attended_ref, bf16[512,8192]{1,0:T(8,128)(2,1)} %weight_hbm.1), custom_call_target="tpu_custom_call" | custom-call | flops 3221225472 | bytes 9568256 | tf_op jit(solution)/shard_map/pallas_call | solution.py:538
  92.3 0.0 copy-done.1
  92.3 0.0 copy-start.2
  92.3 0.4 fusion
  92.7 0.0 copy-start
  92.7 0.3 copy-done.2
  93.0 1.1 %fusion.2 = bf16[48,8192]{1,0:T(8,128)(2,1)} fusion(bf16[48,8192]{1,0:T(8,128)(2,1)S(1)} %get-tuple-element.3, f32[8192]{0:T(1024)S(1)} %copy-done.2, f32[48]{0:T(128)S(1)} %add_sqrt_fusion), kind=kLoop, calls=%fused_computation.4 | loop fusion | flops 1572864 | bytes 1605824 | tf_op jit(solution)/shard_map/convert_element_type | solution.py:591
  94.2 0.0 copy-done
  (1 shorter events, 0.0 us)
Async XLA Ops:
  45.1 47.1 %copy-start.1 = (bf16[48,8192]{1,0:T(8,128)(2,1)S(1)}, bf16[48,8192]{1,0:T(8,128)(2,1)}, u32[]{:S(2)}) copy-start(bf16[48,8192]{1,0:T(8,128)(2,1)} %param.11) | copy-start | bytes 2359300
  92.3 0.8 copy-start.2
  92.7 1.5 %copy-start = (bf16[48,8192]{1,0:T(8,128)(2,1)}, bf16[48,8192]{1,0:T(8,128)(2,1)S(1)}, u32[]{:S(2)}) copy-start(bf16[48,8192]{1,0:T(8,128)(2,1)S(1)} %get-tuple-element.3) | copy-start | bytes 2359300

commit v5 on v4

--- a/solution.py
+++ b/solution.py
@@ -14,15 +14,18 @@
 CORES = 2
 GROUP = Y * CORES
 OWN = 16
-
-
-def exchange_kernel(
+RING = 4
+TP_PARTNERS = 3
+
+
+def exchange(
     heads,
+    begin,
     slot_prompt_ref,
     query_hbm,
     own_hbm,
     cache_hbm,
-    out_ref,
+    attended_ref,
     query_ref,
     own_ref,
     own_rows,
@@ -86,6 +89,7 @@
     ]
     for load in loads:
         load.start()
+    begin()
     barrier = pltpu.get_barrier_semaphore()
 
     def greet(at, carry):
@@ -127,7 +131,7 @@
         ).start()
         return carry
 
-    pl.semaphore_wait(barrier, prompts - 1)
+    pl.semaphore_wait(barrier, prompts - 1 + TP_PARTNERS)
     for group in range(Z_HI):
         lax.fori_loop(max(1, group * GROUP), (group + 1) * GROUP, send_out, 0)
 
@@ -216,51 +220,33 @@
     others = back.at[pl.ds(1, prompts - 1)]
     pltpu.make_async_copy(others, others, back_sem).wait()
 
-    def place(prompt, carry):
-        slot = slot_of[prompt]
+    block_rows = together * rows
+    lines = block_rows * heads
+    at = lax.broadcasted_iota(jnp.int32, (lines, lines), 0)
+    taken = lax.broadcasted_iota(jnp.int32, (lines, lines), 1)
+    wanted = lax.rem(at, block_rows) * heads + at // block_rows
+    move = jnp.where(taken == wanted, 1.0, 0.0).astype(jnp.bfloat16)
+
+    def arrived_from(slot):
         dz = lax.rem(slot // GROUP - here_z + Z_HI, Z_HI)
         dy = lax.rem(lax.rem(slot, GROUP) // CORES - here_y + Y, Y)
         dcore = lax.rem(lax.rem(slot, CORES) + here_core, CORES)
-        out_ref[prompt] = back[z_distance(dz) * GROUP + dy * CORES + dcore]
+        return back[z_distance(dz) * GROUP + dy * CORES + dcore]
+
+    def place(block, carry):
+        pieces = [arrived_from(slot_of[block * together + j]) for j in range(together)]
+        moved = lax.dot_general(
+            move, jnp.concatenate(pieces, axis=0), nn, preferred_element_type=jnp.float32
+        ).astype(jnp.bfloat16)
+        into = pl.ds(pl.multiple_of(block * block_rows, block_rows), block_rows)
+        for head in range(heads):
+            columns = pl.ds(head * head_size, head_size)
+            attended_ref[into, columns] = moved[head * block_rows : (head + 1) * block_rows]
         return carry
 
-    lax.fori_loop(0, prompts, place, 0)
-
-
-def exchange(slot_prompt, query, own_rows, cache, heads):
-    prompts, query_rows, head_size = query.shape
-    width = query_rows + 2 * OWN
-    held = jnp.bfloat16
-    dma = pltpu.SemaphoreType.DMA
-    hbm = pl.BlockSpec(memory_space=pl.ANY)
-    return pl.pallas_call(
-        functools.partial(exchange_kernel, heads),
-        in_specs=[pl.BlockSpec(memory_space=pltpu.SMEM), hbm, hbm, hbm],
-        out_specs=pl.BlockSpec(memory_space=pltpu.VMEM),
-        out_shape=jax.ShapeDtypeStruct(query.shape, held),
-        scratch_shapes=[
-            pltpu.VMEM(query.shape, held),
-            pltpu.VMEM((prompts, OWN, 2 * head_size), held),
-            pltpu.VMEM(own_rows.shape, held),
-            pltpu.VMEM(cache.shape, held),
-            pltpu.VMEM((prompts, width, head_size), held),
-            pltpu.VMEM((prompts, width, head_size), held),
-            pltpu.VMEM(query.shape, held),
-            pltpu.VMEM(query.shape, held),
-            pltpu.SMEM((prompts,), jnp.int32),
-            dma((3,)),
-            dma,
-            dma((Z_HI,)),
-            dma,
-            dma,
-        ],
-        compiler_params=pltpu.CompilerParams(
-            collective_id=1, has_side_effects=True, vmem_limit_bytes=60 * 2**20
-        ),
-    )(slot_prompt, query, own_rows, cache)
-
-
-RING = 4
+    lax.fori_loop(0, prompts // together, place, 0)
+
+
 RING_UNITS = (2, 2, 2, 2, 1)
 PAIR_UNITS = (2, 2, 2, 1)
 RING_FIRST = len(RING_UNITS)
@@ -315,7 +301,7 @@
 )
 
 
-def project_kernel(
+def project(
     attended_ref,
     weight_hbm,
     out_ref,
@@ -489,61 +475,97 @@
         else:
             finish(chunks[(False, k, way)], total)
 
-    for kind, k, _ in ORDER:
-        if kind in (START_RING, START_PAIR):
+    def begin():
+        for kind, k, _ in ORDER:
+            if kind in (START_RING, START_PAIR):
+                for way in range(2):
+                    fetch(chunks[(kind == START_RING, k, way)]).start()
+        barrier = pltpu.get_barrier_semaphore()
+        for device in (ring_device(0), ring_device(1), pair_device):
+            pl.semaphore_signal(
+                barrier, inc=1, device_id=device, device_id_type=pl.DeviceIdType.MESH
+            )
+
+    def run():
+        for kind, k, step in ORDER:
             for way in range(2):
-                fetch(chunks[(kind == START_RING, k, way)]).start()
-    barrier = pltpu.get_barrier_semaphore()
-    for device in (ring_device(0), ring_device(1), pair_device):
-        pl.semaphore_signal(
-            barrier, inc=1, device_id=device, device_id_type=pl.DeviceIdType.MESH
-        )
-    pl.semaphore_wait(barrier, 3)
-
-    for kind, k, step in ORDER:
+                if kind == START_RING:
+                    start_ring(k, way)
+                elif kind == START_PAIR:
+                    start_pair(k, way)
+                elif kind == RING_STEP:
+                    ring_step(k, way, step)
+                elif kind == RING_END:
+                    ring_end(k, way)
+                elif kind == PAIR_STEP:
+                    pair_step(k, way)
+                else:
+                    pair_ring_step(k, way, step)
         for way in range(2):
-            if kind == START_RING:
-                start_ring(k, way)
-            elif kind == START_PAIR:
-                start_pair(k, way)
-            elif kind == RING_STEP:
-                ring_step(k, way, step)
-            elif kind == RING_END:
-                ring_end(k, way)
-            elif kind == PAIR_STEP:
-                pair_step(k, way)
-            else:
-                pair_ring_step(k, way, step)
-    for way in range(2):
-        for k in range(RING_FIRST):
-            for step in range(RING - 1):
-                ring_copy(k, way, step).wait_send()
-            ring_pair_copy(k, way).wait_send()
-        for k in range(PAIR_FIRST):
-            pair_copy(k, way).wait_send()
-            for step in range(RING - 1):
-                pair_ring_copy(k, way, step).wait_send()
-
-
-def project(attended, out_weight):
-    total, depth = attended.shape
-    columns = out_weight.shape[1]
+            for k in range(RING_FIRST):
+                for step in range(RING - 1):
+                    ring_copy(k, way, step).wait_send()
+                ring_pair_copy(k, way).wait_send()
+            for k in range(PAIR_FIRST):
+                pair_copy(k, way).wait_send()
+                for step in range(RING - 1):
+                    pair_ring_copy(k, way, step).wait_send()
+
+    return begin, run
+
+
+def kernel(heads, *refs):
+    inputs, out_ref, scratch = refs[:5], refs[5], refs[6:]
+    slot_prompt_ref, query_hbm, own_hbm, cache_hbm, weight_hbm = inputs
+    attended_ref, exchange_scratch, project_scratch = scratch[0], scratch[1:15], scratch[15:]
+    begin, run = project(attended_ref, weight_hbm, out_ref, *project_scratch)
+    exchange(
+        heads,
+        begin,
+        slot_prompt_ref,
+        query_hbm,
+        own_hbm,
+        cache_hbm,
+        attended_ref,
+        *exchange_scratch,
+    )
+    run()
+
+
+def attend_and_project(slot_prompt, query, own_rows, cache, out_weight, heads):
+    prompts, query_rows, head_size = query.shape
+    message = query_rows + 2 * OWN
+    held = jnp.bfloat16
+    dma = pltpu.SemaphoreType.DMA
+    hbm = pl.BlockSpec(memory_space=pl.ANY)
+    depth, columns = out_weight.shape
+    total = own_rows.shape[0]
     rows = total // (2 * RING)
     chunks = 2 * (RING_FIRST + PAIR_FIRST)
     units = 2 * (sum(RING_UNITS) + sum(PAIR_UNITS))
     width = max(RING_UNITS + PAIR_UNITS) * columns // units
     steps = RING - 1
-    dma = pltpu.SemaphoreType.DMA
-    held = jnp.bfloat16
     return pl.pallas_call(
-        project_kernel,
-        in_specs=[
-            pl.BlockSpec(memory_space=pltpu.VMEM),
-            pl.BlockSpec(memory_space=pl.ANY),
-        ],
+        functools.partial(kernel, heads),
+        in_specs=[pl.BlockSpec(memory_space=pltpu.SMEM), hbm, hbm, hbm, hbm],
         out_specs=pl.BlockSpec(memory_space=pltpu.VMEM),
         out_shape=jax.ShapeDtypeStruct((rows, columns), held),
         scratch_shapes=[
+            pltpu.VMEM((total, depth), held),
+            pltpu.VMEM(query.shape, held),
+            pltpu.VMEM((prompts, OWN, 2 * head_size), held),
+            pltpu.VMEM(own_rows.shape, held),
+            pltpu.VMEM(cache.shape, held),
+            pltpu.VMEM((prompts, message, head_size), held),
+            pltpu.VMEM((prompts, message, head_size), held),
+            pltpu.VMEM(query.shape, held),
+            pltpu.VMEM(query.shape, held),
+            pltpu.SMEM((prompts,), jnp.int32),
+            dma((3,)),
+            dma,
+            dma((Z_HI,)),
+            dma,
+            dma,
             pltpu.VMEM((chunks, depth, width), held),
             dma((chunks,)),
             pltpu.VMEM((2, RING_FIRST, RING, 2, rows, width), held),
@@ -562,29 +584,23 @@
             dma((2, PAIR_FIRST, steps)),
         ],
         compiler_params=pltpu.CompilerParams(
-            collective_id=0, has_side_effects=True, vmem_limit_bytes=48 * 2**20
+            collective_id=0, has_side_effects=True, vmem_limit_bytes=60 * 2**20
         ),
-        cost_estimate=pl.CostEstimate(
-            flops=2 * total * depth * columns,
-            bytes_accessed=2 * (depth * columns + total * depth + rows * columns),
-            transcendentals=0,
-        ),
-    )(attended, out_weight)
+    )(slot_prompt, query, own_rows, cache, out_weight)
 
 
 def on_device(queries, cache, new_kv, slot_prompt, residual, out_weight, gain):
     row_total, heads_local, head_size = queries.shape
     prompts = slot_prompt.shape[0]
     rows = row_total // prompts
-    attended = exchange(
+    projected = attend_and_project(
         slot_prompt,
         queries.reshape(prompts, rows * heads_local, head_size),
         new_kv.reshape(row_total, 2 * head_size),
         cache.reshape(cache.shape[1], 2 * head_size),
+        out_weight,
         heads_local,
-    )
-    attended = attended.reshape(row_total, heads_local * head_size)
-    projected = project(attended, out_weight).astype(jnp.float32)
+    ).astype(jnp.float32)
     hidden = (residual.astype(jnp.float32) + projected).astype(jnp.bfloat16)
     hidden_f = hidden.astype(jnp.float32)
     spread = jnp.sqrt(jnp.mean(hidden_f * hidden_f, -1) + 1e-05)

time: 95.6 us -> 94.8 us (level)
  local copies, waits for them, and re-layouts: 1.59 us -> 0.02 us
  other arithmetic: 1.52 us -> 2.66 us
    reshape x1 -> x0, local copies, waits for them, and re-layouts: 1.24 us -> none  [on_device(): attended = attended.reshape(row_total, heads_local * head_size)]
    reduce_sum x1, other arithmetic: 0.38 us -> 1.52 us  [on_device(): spread = jnp.sqrt(jnp.mean(hidden_f * hidden_f, -1) + 1e-05)]
    pallas_call x2 -> x1, Pallas kernels: 90.4 us -> 90.7 us  [attend_and_project(): pl.pallas_call(functools.partial(kernel, heads), in_specs=[pl.BlockSpec(m...]
where the time goes in v5:
time: 94.8 us; the launch traced here: 94 us
  Pallas kernels  90.7 us (96%)
  other arithmetic  2.66 us (3%)
    pallas_call x1, Pallas kernels, attend_and_project(): pl.pallas_call(functools.partial(kernel, heads), in_specs=[pl.BlockSpec(m...  90.7 us

profile of v5, /device:TPU:1, one launch (start us, length us, event | category | flops | bytes accessed | tf_op | source)
XLA Modules:
  0.0 94.0 jit_solution(16537202653534433672)
XLA Ops:
  0.6 0.0 copy-start.1
  0.6 90.7 %shard_map.86 = bf16[48,8192]{1,0:T(8,128)(2,1)} custom-call(s32[32]{0:T(128)} %refs_0_.1, bf16[32,48,128]{2,1,0:T(8,128)(2,1)} %bitcast.4, bf16[384,256]{1,0:T(8,128)(2,1)} %bitcast.5, bf16[1024,256]{1,0:T(8,128)(2,1)} %bitcast.3, bf16[512,8192]{1,0:T(8,128)(2,1)} %refs_4_.1), custom_call_target="tpu_custom_call" | custom-call | tf_op jit(solution)/shard_map/pallas_call | solution.py:548
  91.3 0.0 copy-done.1
  91.3 0.0 copy-start.2
  91.3 1.5 %fusion = (f32[48]{0:T(128)S(1)}, bf16[48,8192]{1,0:T(8,128)(2,1)S(1)}) fusion(bf16[48,8192]{1,0:T(8,128)(2,1)} %shard_map.86, bf16[48,8192]{1,0:T(8,128)(2,1)S(1)} %copy-done.1), kind=kLoop, calls=%fused_computation.2 | loop fusion | flops 2752464 | bytes 2359488 | tf_op jit(solution)/shard_map/reduce_sum | solution.py:606
  92.9 0.0 copy-start
  92.9 0.0 copy-done.2
  92.9 1.1 %fusion.2 = bf16[48,8192]{1,0:T(8,128)(2,1)} fusion(bf16[48,8192]{1,0:T(8,128)(2,1)S(1)} %get-tuple-element.3, f32[8192]{0:T(1024)S(1)} %copy-done.2, f32[48]{0:T(128)S(1)} %add_sqrt_fusion), kind=kLoop, calls=%fused_computation.4 | loop fusion | flops 1572864 | bytes 1605824 | tf_op jit(solution)/shard_map/convert_element_type | solution.py:607
  94.0 0.0 copy-done
  (1 shorter events, 0.0 us)
Async XLA Ops:
  0.6 90.7 %copy-start.1 = (bf16[48,8192]{1,0:T(8,128)(2,1)S(1)}, bf16[48,8192]{1,0:T(8,128)(2,1)}, u32[]{:S(2)}) copy-start(bf16[48,8192]{1,0:T(8,128)(2,1)} %param.11) | copy-start | bytes 2359300
  91.3 1.6 %copy-start.2 = (f32[8192]{0:T(1024)S(1)}, f32[8192]{0:T(1024)}, u32[]{:S(2)}) copy-start(f32[8192]{0:T(1024)} %param.13) | copy-start | bytes 98308
  92.9 1.2 %copy-start = (bf16[48,8192]{1,0:T(8,128)(2,1)}, bf16[48,8192]{1,0:T(8,128)(2,1)S(1)}, u32[]{:S(2)}) copy-start(bf16[48,8192]{1,0:T(8,128)(2,1)S(1)} %get-tuple-element.3) | copy-start | bytes 2359300

commit v6 on v5

--- a/solution.py
+++ b/solution.py
@@ -34,7 +34,7 @@
     held,
     done,
     back,
-    slot_of,
+    offset_of,
     load_sem,
     sent_sem,
     held_sem,
@@ -132,14 +132,18 @@
         return carry
 
     pl.semaphore_wait(barrier, prompts - 1 + TP_PARTNERS)
-    for group in range(Z_HI):
+    for group in (3, 1, 2, 0):
         lax.fori_loop(max(1, group * GROUP), (group + 1) * GROUP, send_out, 0)
 
     def find(prompt, carry):
         def look(slot, found):
             return jnp.where(slot_prompt_ref[slot] == prompt, slot, found)
 
-        slot_of[prompt] = lax.fori_loop(0, prompts, look, 0)
+        slot = lax.fori_loop(0, prompts, look, 0)
+        dz = lax.rem(slot // GROUP - here_z + Z_HI, Z_HI)
+        dy = lax.rem(lax.rem(slot, GROUP) // CORES - here_y + Y, Y)
+        dcore = lax.rem(lax.rem(slot, CORES) + here_core, CORES)
+        offset_of[prompt] = z_distance(dz) * GROUP + dy * CORES + dcore
         return carry
 
     lax.fori_loop(0, prompts, find, 0)
@@ -205,14 +209,13 @@
 
         lax.fori_loop(start, base + GROUP, send_back, 0)
 
+    def attend_next(step, carry):
+        attend(lax.rem(step + 2, Z_HI - 1) + 1, False)
+        return carry
+
     loads[2].wait()
+    lax.fori_loop(0, Z_HI - 1, attend_next, 0)
     attend(0, True)
-
-    def attend_next(group, carry):
-        attend(group, False)
-        return carry
-
-    lax.fori_loop(1, Z_HI, attend_next, 0)
     others = sent.at[pl.ds(1, prompts - 1)]
     pltpu.make_async_copy(others, others, sent_sem).wait()
     others = done.at[pl.ds(1, prompts - 1)]
@@ -227,14 +230,8 @@
     wanted = lax.rem(at, block_rows) * heads + at // block_rows
     move = jnp.where(taken == wanted, 1.0, 0.0).astype(jnp.bfloat16)
 
-    def arrived_from(slot):
-        dz = lax.rem(slot // GROUP - here_z + Z_HI, Z_HI)
-        dy = lax.rem(lax.rem(slot, GROUP) // CORES - here_y + Y, Y)
-        dcore = lax.rem(lax.rem(slot, CORES) + here_core, CORES)
-        return back[z_distance(dz) * GROUP + dy * CORES + dcore]
-
     def place(block, carry):
-        pieces = [arrived_from(slot_of[block * together + j]) for j in range(together)]
+        pieces = [back[offset_of[block * together + j]] for j in range(together)]
         moved = lax.dot_general(
             move, jnp.concatenate(pieces, axis=0), nn, preferred_element_type=jnp.float32
         ).astype(jnp.bfloat16)
@@ -304,7 +301,14 @@
 def project(
     attended_ref,
     weight_hbm,
-    out_ref,
+    residual_hbm,
+    gain_hbm,
+    hidden_ref,
+    normed_ref,
+    residual,
+    gain,
+    squares,
+    row_sem,
     weight,
     weight_sem,
     xp,
@@ -322,7 +326,7 @@
     zr_send,
     zr_recv,
 ):
-    rows = out_ref.shape[0]
+    rows, columns_total = hidden_ref.shape
     here = lax.axis_index("tp")
     x = lax.rem(here, RING)
     z = here // RING
@@ -338,7 +342,7 @@
         ahead = 2 * RING - 1 - step if way == 0 else 1 + step
         return lax.rem(x + ahead, RING)
 
-    unit = out_ref.shape[1] // (2 * (sum(RING_UNITS) + sum(PAIR_UNITS)))
+    unit = columns_total // (2 * (sum(RING_UNITS) + sum(PAIR_UNITS)))
     chunks = {}
     start = 0
     for units in (RING_UNITS, PAIR_UNITS):
@@ -434,7 +438,15 @@
 
     def finish(chunk, total):
         _, start, width = chunk
-        out_ref[:, start : start + width] = total.astype(jnp.bfloat16)
+        columns = slice(start, start + width)
+        hidden = (wide(residual[:, columns]) + total).astype(jnp.bfloat16)
+        hidden_ref[:, columns] = hidden
+        square = wide(hidden) * wide(hidden)
+        lanes = squares.shape[1]
+        found = squares[...]
+        for at in range(0, width, lanes):
+            found = found + square[:, at : at + lanes]
+        squares[...] = found
 
     def ring_step(k, way, step):
         ring_copy(k, way, step).wait_recv()
@@ -475,11 +487,18 @@
         else:
             finish(chunks[(False, k, way)], total)
 
+    row_loads = [
+        pltpu.make_async_copy(residual_hbm, residual, row_sem.at[0]),
+        pltpu.make_async_copy(gain_hbm, gain, row_sem.at[1]),
+    ]
+
     def begin():
         for kind, k, _ in ORDER:
             if kind in (START_RING, START_PAIR):
                 for way in range(2):
                     fetch(chunks[(kind == START_RING, k, way)]).start()
+        for load in row_loads:
+            load.start()
         barrier = pltpu.get_barrier_semaphore()
         for device in (ring_device(0), ring_device(1), pair_device):
             pl.semaphore_signal(
@@ -487,6 +506,9 @@
             )
 
     def run():
+        for load in row_loads:
+            load.wait()
+        squares[...] = jnp.zeros_like(squares)
         for kind, k, step in ORDER:
             for way in range(2):
                 if kind == START_RING:
@@ -501,6 +523,13 @@
                     pair_step(k, way)
                 else:
                     pair_ring_step(k, way, step)
+        mean = jnp.sum(squares[...], -1, keepdims=True) / columns_total
+        inverse = 1.0 / jnp.sqrt(mean + 1e-05)
+        part = 2 * unit
+        for at in range(0, columns_total, part):
+            columns = slice(at, at + part)
+            normed = wide(hidden_ref[:, columns]) * inverse * gain[:, columns]
+            normed_ref[:, columns] = normed.astype(jnp.bfloat16)
         for way in range(2):
             for k in range(RING_FIRST):
                 for step in range(RING - 1):
@@ -515,10 +544,10 @@
 
 
 def kernel(heads, *refs):
-    inputs, out_ref, scratch = refs[:5], refs[5], refs[6:]
-    slot_prompt_ref, query_hbm, own_hbm, cache_hbm, weight_hbm = inputs
+    inputs, outputs, scratch = refs[:7], refs[7:9], refs[9:]
+    slot_prompt_ref, query_hbm, own_hbm, cache_hbm = inputs[:4]
     attended_ref, exchange_scratch, project_scratch = scratch[0], scratch[1:15], scratch[15:]
-    begin, run = project(attended_ref, weight_hbm, out_ref, *project_scratch)
+    begin, run = project(attended_ref, *inputs[4:], *outputs, *project_scratch)
     exchange(
         heads,
         begin,
@@ -532,7 +561,7 @@
     run()
 
 
-def attend_and_project(slot_prompt, query, own_rows, cache, out_weight, heads):
+def attend_and_project(slot_prompt, query, own_rows, cache, out_weight, residual, gain, heads):
     prompts, query_rows, head_size = query.shape
     message = query_rows + 2 * OWN
     held = jnp.bfloat16
@@ -547,9 +576,9 @@
     steps = RING - 1
     return pl.pallas_call(
         functools.partial(kernel, heads),
-        in_specs=[pl.BlockSpec(memory_space=pltpu.SMEM), hbm, hbm, hbm, hbm],
-        out_specs=pl.BlockSpec(memory_space=pltpu.VMEM),
-        out_shape=jax.ShapeDtypeStruct((rows, columns), held),
+        in_specs=[pl.BlockSpec(memory_space=pltpu.SMEM)] + [hbm] * 6,
+        out_specs=[pl.BlockSpec(memory_space=pltpu.VMEM)] * 2,
+        out_shape=[jax.ShapeDtypeStruct((rows, columns), held)] * 2,
         scratch_shapes=[
             pltpu.VMEM((total, depth), held),
             pltpu.VMEM(query.shape, held),
@@ -566,6 +595,10 @@
             dma((Z_HI,)),
             dma,
             dma,
+            pltpu.VMEM(residual.shape, held),
+            pltpu.VMEM(gain.shape, jnp.float32),
+            pltpu.VMEM((rows, 128), jnp.float32),
+            dma((2,)),
             pltpu.VMEM((chunks, depth, width), held),
             dma((chunks,)),
             pltpu.VMEM((2, RING_FIRST, RING, 2, rows, width), held),
@@ -586,25 +619,23 @@
         compiler_params=pltpu.CompilerParams(
             collective_id=0, has_side_effects=True, vmem_limit_bytes=60 * 2**20
         ),
-    )(slot_prompt, query, own_rows, cache, out_weight)
+    )(slot_prompt, query, own_rows, cache, out_weight, residual, gain)
 
 
 def on_device(queries, cache, new_kv, slot_prompt, residual, out_weight, gain):
     row_total, heads_local, head_size = queries.shape
     prompts = slot_prompt.shape[0]
     rows = row_total // prompts
-    projected = attend_and_project(
+    hidden, normed = attend_and_project(
         slot_prompt,
         queries.reshape(prompts, rows * heads_local, head_size),
         new_kv.reshape(row_total, 2 * head_size),
         cache.reshape(cache.shape[1], 2 * head_size),
         out_weight,
+        residual,
+        gain[None, :],
         heads_local,
-    ).astype(jnp.float32)
-    hidden = (residual.astype(jnp.float32) + projected).astype(jnp.bfloat16)
-    hidden_f = hidden.astype(jnp.float32)
-    spread = jnp.sqrt(jnp.mean(hidden_f * hidden_f, -1) + 1e-05)
-    normed = (hidden_f / spread[:, None] * gain[None, :]).astype(jnp.bfloat16)
+    )
     return (hidden, normed)
 
 

time: 94.8 us -> 95.4 us (level)
  local copies, waits for them, and re-layouts: 0.02 us -> 4.13 us
  other arithmetic: 2.66 us -> 0 us
    unnamed x6 -> x2, local copies, waits for them, and re-layouts: 0.02 us -> 4.13 us
    reduce_sum x1 -> x0, other arithmetic: 1.52 us -> none  [on_device(): spread = jnp.sqrt(jnp.mean(hidden_f * hidden_f, -1) + 1e-05)]
    convert_element_type x1 -> x0, other arithmetic: 1.14 us -> none  [on_device(): normed = (hidden_f / spread[:, None] * gain[None, :]).astype(jnp.bfloat16)]
where the time goes in v6:
time: 95.4 us; the launch traced here: 94.6 us
  Pallas kernels  89.8 us (94%)
  local copies, waits for them, and re-layouts  4.13 us (4%)
    pallas_call x1, Pallas kernels, attend_and_project(): pl.pallas_call(functools.partial(kernel, heads), in_specs=[pl.BlockSpec(m...  89.8 us
    unnamed x2, local copies, waits for them, and re-layouts  4.13 us

profile of v6, /device:TPU:1, one launch (start us, length us, event | category | flops | bytes accessed | tf_op | source)
XLA Modules:
  0.0 94.6 jit_solution(998107909713476898)
XLA Ops:
  0.6 89.8 %shard_map.86 = (bf16[48,8192]{1,0:T(8,128)(2,1)}, bf16[48,8192]{1,0:T(8,128)(2,1)}) custom-call(s32[32]{0:T(128)} %refs_0_.1, bf16[32,48,128]{2,1,0:T(8,128)(2,1)} %bitcast.5, bf16[384,256]{1,0:T(8,128)(2,1)} %bitcast.6, bf16[1024,256]{1,0:T(8,128)(2,1)} %bitcast.4, bf16[512,8192]{1,0:T(8,128)(2,1)} %refs_4_.1, bf16[48,8192]{1,0:T(8,128)(2,1)} %refs_5_.1, ...), custom_call_target="tpu_custom_call" | custom-call | tf_op jit(solution)/shard_map/pallas_call | solution.py:577
  90.5 2.1 %copy.11 = bf16[48,8192]{1,0:T(8,128)(2,1)} copy(bf16[48,8192]{1,0:T(8,128)(2,1)} %get-tuple-element.4) | data formatting | bytes 1572864
  92.5 2.1 %copy.12 = bf16[48,8192]{1,0:T(8,128)(2,1)} copy(bf16[48,8192]{1,0:T(8,128)(2,1)} %get-tuple-element.5) | data formatting | bytes 1572864

commit v7 on v6

--- a/solution.py
+++ b/solution.py
@@ -302,11 +302,9 @@
     attended_ref,
     weight_hbm,
     residual_hbm,
-    gain_hbm,
-    hidden_ref,
-    normed_ref,
+    projected_ref,
+    inverse_ref,
     residual,
-    gain,
     squares,
     row_sem,
     weight,
@@ -326,7 +324,7 @@
     zr_send,
     zr_recv,
 ):
-    rows, columns_total = hidden_ref.shape
+    rows, columns_total = projected_ref.shape
     here = lax.axis_index("tp")
     x = lax.rem(here, RING)
     z = here // RING
@@ -439,8 +437,9 @@
     def finish(chunk, total):
         _, start, width = chunk
         columns = slice(start, start + width)
-        hidden = (wide(residual[:, columns]) + total).astype(jnp.bfloat16)
-        hidden_ref[:, columns] = hidden
+        projected = total.astype(jnp.bfloat16)
+        projected_ref[:, columns] = projected
+        hidden = (wide(residual[:, columns]) + wide(projected)).astype(jnp.bfloat16)
         square = wide(hidden) * wide(hidden)
         lanes = squares.shape[1]
         found = squares[...]
@@ -487,18 +486,14 @@
         else:
             finish(chunks[(False, k, way)], total)
 
-    row_loads = [
-        pltpu.make_async_copy(residual_hbm, residual, row_sem.at[0]),
-        pltpu.make_async_copy(gain_hbm, gain, row_sem.at[1]),
-    ]
+    row_load = pltpu.make_async_copy(residual_hbm, residual, row_sem)
 
     def begin():
         for kind, k, _ in ORDER:
             if kind in (START_RING, START_PAIR):
                 for way in range(2):
                     fetch(chunks[(kind == START_RING, k, way)]).start()
-        for load in row_loads:
-            load.start()
+        row_load.start()
         barrier = pltpu.get_barrier_semaphore()
         for device in (ring_device(0), ring_device(1), pair_device):
             pl.semaphore_signal(
@@ -506,8 +501,7 @@
             )
 
     def run():
-        for load in row_loads:
-            load.wait()
+        row_load.wait()
         squares[...] = jnp.zeros_like(squares)
         for kind, k, step in ORDER:
             for way in range(2):
@@ -524,12 +518,7 @@
                 else:
                     pair_ring_step(k, way, step)
         mean = jnp.sum(squares[...], -1, keepdims=True) / columns_total
-        inverse = 1.0 / jnp.sqrt(mean + 1e-05)
-        part = 2 * unit
-        for at in range(0, columns_total, part):
-            columns = slice(at, at + part)
-            normed = wide(hidden_ref[:, columns]) * inverse * gain[:, columns]
-            normed_ref[:, columns] = normed.astype(jnp.bfloat16)
+        inverse_ref[...] = jnp.broadcast_to(1.0 / jnp.sqrt(mean + 1e-05), inverse_ref.shape)
         for way in range(2):
             for k in range(RING_FIRST):
                 for step in range(RING - 1):
@@ -544,7 +533,7 @@
 
 
 def kernel(heads, *refs):
-    inputs, outputs, scratch = refs[:7], refs[7:9], refs[9:]
+    inputs, outputs, scratch = refs[:6], refs[6:8], refs[8:]
     slot_prompt_ref, query_hbm, own_hbm, cache_hbm = inputs[:4]
     attended_ref, exchange_scratch, project_scratch = scratch[0], scratch[1:15], scratch[15:]
     begin, run = project(attended_ref, *inputs[4:], *outputs, *project_scratch)
@@ -561,7 +550,7 @@
     run()
 
 
-def attend_and_project(slot_prompt, query, own_rows, cache, out_weight, residual, gain, heads):
+def attend_and_project(slot_prompt, query, own_rows, cache, out_weight, residual, heads):
     prompts, query_rows, head_size = query.shape
     message = query_rows + 2 * OWN
     held = jnp.bfloat16
@@ -576,9 +565,12 @@
     steps = RING - 1
     return pl.pallas_call(
         functools.partial(kernel, heads),
-        in_specs=[pl.BlockSpec(memory_space=pltpu.SMEM)] + [hbm] * 6,
+        in_specs=[pl.BlockSpec(memory_space=pltpu.SMEM)] + [hbm] * 5,
         out_specs=[pl.BlockSpec(memory_space=pltpu.VMEM)] * 2,
-        out_shape=[jax.ShapeDtypeStruct((rows, columns), held)] * 2,
+        out_shape=[
+            jax.ShapeDtypeStruct((rows, columns), held),
+            jax.ShapeDtypeStruct((rows, 128), jnp.float32),
+        ],
         scratch_shapes=[
             pltpu.VMEM((total, depth), held),
             pltpu.VMEM(query.shape, held),
@@ -596,9 +588,8 @@
             dma,
             dma,
             pltpu.VMEM(residual.shape, held),
-            pltpu.VMEM(gain.shape, jnp.float32),
             pltpu.VMEM((rows, 128), jnp.float32),
-            dma((2,)),
+            dma,
             pltpu.VMEM((chunks, depth, width), held),
             dma((chunks,)),
             pltpu.VMEM((2, RING_FIRST, RING, 2, rows, width), held),
@@ -619,24 +610,26 @@
         compiler_params=pltpu.CompilerParams(
             collective_id=0, has_side_effects=True, vmem_limit_bytes=60 * 2**20
         ),
-    )(slot_prompt, query, own_rows, cache, out_weight, residual, gain)
+    )(slot_prompt, query, own_rows, cache, out_weight, residual)
 
 
 def on_device(queries, cache, new_kv, slot_prompt, residual, out_weight, gain):
     row_total, heads_local, head_size = queries.shape
     prompts = slot_prompt.shape[0]
     rows = row_total // prompts
-    hidden, normed = attend_and_project(
+    projected, inverse = attend_and_project(
         slot_prompt,
         queries.reshape(prompts, rows * heads_local, head_size),
         new_kv.reshape(row_total, 2 * head_size),
         cache.reshape(cache.shape[1], 2 * head_size),
         out_weight,
         residual,
-        gain[None, :],
         heads_local,
     )
-    return (hidden, normed)
+    hidden = residual.astype(jnp.float32) + projected.astype(jnp.float32)
+    hidden = hidden.astype(jnp.bfloat16)
+    normed = hidden.astype(jnp.float32) * inverse[:, :1] * gain[None, :]
+    return (hidden, normed.astype(jnp.bfloat16))
 
 
 def solution(mesh):

time: 95.4 us -> 94.5 us (level)
  local copies, waits for them, and re-layouts: 4.13 us -> 0.85 us
  other arithmetic: 0 us -> 2.62 us
    unnamed x2 -> x4, local copies, waits for them, and re-layouts: 4.13 us -> 0.01 us
    convert_element_type x0 -> x1, other arithmetic: none -> 2.62 us  [on_device(): return (hidden, normed.astype(jnp.bfloat16))]
where the time goes in v7:
time: 94.5 us; the launch traced here: 93.6 us
  Pallas kernels  89.5 us (95%)
  other arithmetic  2.62 us (3%)
    pallas_call x1, Pallas kernels, attend_and_project(): pl.pallas_call(functools.partial(kernel, heads), in_specs=[pl.BlockSpec(m...  89.5 us
    convert_element_type x1, other arithmetic, on_device(): return (hidden, normed.astype(jnp.bfloat16))  2.62 us

profile of v7, /device:TPU:1, one launch (start us, length us, event | category | flops | bytes accessed | tf_op | source)
XLA Modules:
  0.0 93.6 jit_solution(14089403092909140398)
XLA Ops:
  0.6 0.0 copy-start
  0.6 0.0 copy-start.1
  0.7 89.5 %shard_map.86 = (bf16[48,8192]{1,0:T(8,128)(2,1)}, f32[48,128]{1,0:T(8,128)}) custom-call(s32[32]{0:T(128)} %refs_0_.1, bf16[32,48,128]{2,1,0:T(8,128)(2,1)} %bitcast.4, bf16[384,256]{1,0:T(8,128)(2,1)} %bitcast.5, bf16[1024,256]{1,0:T(8,128)(2,1)} %bitcast.3, bf16[512,8192]{1,0:T(8,128)(2,1)} %refs_4_.1, bf16[48,8192]{1,0:T(8,128)(2,1)} %refs_5_.1), custom_call_target="tpu_custom_call" | custom-call | tf_op jit(solution)/shard_map/pallas_call | solution.py:566
  90.2 0.8 slice_reduce_fusion
  91.0 0.0 copy-done
  91.0 0.0 copy-done.1
  91.0 2.6 %multiply_convert_fusion = (bf16[48,8192]{1,0:T(8,128)(2,1)}, bf16[48,8192]{1,0:T(8,128)(2,1)}) fusion(f32[8192]{0:T(1024)S(1)} %copy-done.1, f32[48]{0:T(128)S(1)} %slice_reduce_fusion, bf16[48,8192]{1,0:T(8,128)(2,1)} %get-tuple-element.4, bf16[48,8192]{1,0:T(8,128)(2,1)S(1)} %copy-done), kind=kLoop, calls=%fused_computation | loop fusion | flops 3145728 | bytes 3178688 | tf_op jit(solution)/shard_map/convert_element_type | solution.py:632
Async XLA Ops:
  0.6 90.4 %copy-start = (bf16[48,8192]{1,0:T(8,128)(2,1)S(1)}, bf16[48,8192]{1,0:T(8,128)(2,1)}, u32[]{:S(2)}) copy-start(bf16[48,8192]{1,0:T(8,128)(2,1)} %refs_5_.1) | copy-start | bytes 2359300
  0.6 90.4 %copy-start.1 = (f32[8192]{0:T(1024)S(1)}, f32[8192]{0:T(1024)}, u32[]{:S(2)}) copy-start(f32[8192]{0:T(1024)} %param.13) | copy-start | bytes 98308

commit v8 on v5

--- a/solution.py
+++ b/solution.py
@@ -34,7 +34,7 @@
     held,
     done,
     back,
-    slot_of,
+    offset_of,
     load_sem,
     sent_sem,
     held_sem,
@@ -132,14 +132,18 @@
         return carry
 
     pl.semaphore_wait(barrier, prompts - 1 + TP_PARTNERS)
-    for group in range(Z_HI):
+    for group in (3, 1, 2, 0):
         lax.fori_loop(max(1, group * GROUP), (group + 1) * GROUP, send_out, 0)
 
     def find(prompt, carry):
         def look(slot, found):
             return jnp.where(slot_prompt_ref[slot] == prompt, slot, found)
 
-        slot_of[prompt] = lax.fori_loop(0, prompts, look, 0)
+        slot = lax.fori_loop(0, prompts, look, 0)
+        dz = lax.rem(slot // GROUP - here_z + Z_HI, Z_HI)
+        dy = lax.rem(lax.rem(slot, GROUP) // CORES - here_y + Y, Y)
+        dcore = lax.rem(lax.rem(slot, CORES) + here_core, CORES)
+        offset_of[prompt] = z_distance(dz) * GROUP + dy * CORES + dcore
         return carry
 
     lax.fori_loop(0, prompts, find, 0)
@@ -205,14 +209,13 @@
 
         lax.fori_loop(start, base + GROUP, send_back, 0)
 
+    def attend_next(step, carry):
+        attend(lax.rem(step + 2, Z_HI - 1) + 1, False)
+        return carry
+
     loads[2].wait()
+    lax.fori_loop(0, Z_HI - 1, attend_next, 0)
     attend(0, True)
-
-    def attend_next(group, carry):
-        attend(group, False)
-        return carry
-
-    lax.fori_loop(1, Z_HI, attend_next, 0)
     others = sent.at[pl.ds(1, prompts - 1)]
     pltpu.make_async_copy(others, others, sent_sem).wait()
     others = done.at[pl.ds(1, prompts - 1)]
@@ -227,14 +230,8 @@
     wanted = lax.rem(at, block_rows) * heads + at // block_rows
     move = jnp.where(taken == wanted, 1.0, 0.0).astype(jnp.bfloat16)
 
-    def arrived_from(slot):
-        dz = lax.rem(slot // GROUP - here_z + Z_HI, Z_HI)
-        dy = lax.rem(lax.rem(slot, GROUP) // CORES - here_y + Y, Y)
-        dcore = lax.rem(lax.rem(slot, CORES) + here_core, CORES)
-        return back[z_distance(dz) * GROUP + dy * CORES + dcore]
-
     def place(block, carry):
-        pieces = [arrived_from(slot_of[block * together + j]) for j in range(together)]
+        pieces = [back[offset_of[block * together + j]] for j in range(together)]
         moved = lax.dot_general(
             move, jnp.concatenate(pieces, axis=0), nn, preferred_element_type=jnp.float32
         ).astype(jnp.bfloat16)
@@ -254,50 +251,50 @@
 START_RING, START_PAIR, RING_STEP, RING_END, PAIR_STEP, PAIR_RING = range(6)
 ORDER = (
     (START_RING, 4, 0),
+    (START_RING, 1, 0),
     (START_PAIR, 3, 0),
-    (START_RING, 2, 0),
-    (START_RING, 1, 0),
-    (RING_STEP, 4, 0),
-    (START_PAIR, 2, 0),
+    (START_RING, 3, 0),
+    (START_PAIR, 0, 0),
+    (START_PAIR, 1, 0),
+    (RING_STEP, 1, 0),
     (PAIR_STEP, 3, 0),
     (START_RING, 0, 0),
+    (RING_STEP, 4, 0),
+    (RING_STEP, 3, 0),
+    (RING_STEP, 1, 1),
+    (PAIR_RING, 3, 0),
+    (START_PAIR, 2, 0),
+    (START_RING, 2, 0),
+    (RING_STEP, 0, 0),
+    (PAIR_STEP, 0, 0),
     (RING_STEP, 4, 1),
-    (START_PAIR, 1, 0),
-    (RING_STEP, 1, 0),
-    (START_PAIR, 0, 0),
-    (PAIR_RING, 3, 0),
-    (START_RING, 3, 0),
+    (RING_STEP, 3, 1),
+    (RING_STEP, 1, 2),
+    (PAIR_RING, 3, 1),
+    (RING_STEP, 0, 1),
+    (RING_STEP, 2, 0),
+    (PAIR_STEP, 1, 0),
+    (RING_STEP, 4, 2),
+    (PAIR_RING, 0, 0),
+    (RING_STEP, 3, 2),
+    (PAIR_RING, 3, 2),
+    (RING_STEP, 0, 2),
+    (RING_STEP, 2, 1),
     (PAIR_STEP, 2, 0),
-    (RING_STEP, 0, 0),
-    (RING_STEP, 4, 2),
-    (RING_STEP, 2, 0),
-    (RING_STEP, 1, 1),
-    (PAIR_RING, 3, 1),
-    (RING_STEP, 3, 0),
-    (RING_STEP, 0, 1),
-    (PAIR_RING, 2, 0),
-    (PAIR_STEP, 1, 0),
-    (RING_STEP, 2, 1),
-    (RING_STEP, 1, 2),
-    (PAIR_RING, 3, 2),
-    (RING_STEP, 3, 1),
-    (RING_STEP, 0, 2),
-    (PAIR_STEP, 0, 0),
-    (PAIR_RING, 2, 1),
     (PAIR_RING, 1, 0),
+    (PAIR_RING, 0, 1),
+    (RING_END, 1, 0),
     (RING_STEP, 2, 2),
     (RING_END, 4, 0),
-    (RING_END, 1, 0),
-    (RING_STEP, 3, 2),
+    (PAIR_RING, 2, 0),
+    (PAIR_RING, 1, 1),
+    (RING_END, 3, 0),
+    (PAIR_RING, 0, 2),
+    (PAIR_RING, 2, 1),
     (RING_END, 0, 0),
-    (PAIR_RING, 0, 0),
+    (PAIR_RING, 1, 2),
+    (RING_END, 2, 0),
     (PAIR_RING, 2, 2),
-    (PAIR_RING, 1, 1),
-    (RING_END, 2, 0),
-    (PAIR_RING, 0, 1),
-    (RING_END, 3, 0),
-    (PAIR_RING, 1, 2),
-    (PAIR_RING, 0, 2),
 )
 
 

time: 94.8 us -> 93 us (0.981)
  Pallas kernels: 90.7 us -> 88.8 us
    pallas_call x1, Pallas kernels: 90.7 us -> 88.8 us  [attend_and_project(): pl.pallas_call(functools.partial(kernel, heads), in_specs=[pl.BlockSpec(m...]
where the time goes in v8:
time: 93 us; the launch traced here: 92.1 us
  Pallas kernels  88.8 us (95%)
  other arithmetic  2.66 us (3%)
    pallas_call x1, Pallas kernels, attend_and_project(): pl.pallas_call(functools.partial(kernel, heads), in_specs=[pl.BlockSpec(m...  88.8 us

profile of v8, /device:TPU:1, one launch (start us, length us, event | category | flops | bytes accessed | tf_op | source)
XLA Modules:
  0.0 92.1 jit_solution(11660801129767206344)
XLA Ops:
  0.6 0.0 copy-start.1
  0.6 88.8 %shard_map.86 = bf16[48,8192]{1,0:T(8,128)(2,1)} custom-call(s32[32]{0:T(128)} %refs_0_.1, bf16[32,48,128]{2,1,0:T(8,128)(2,1)} %bitcast.4, bf16[384,256]{1,0:T(8,128)(2,1)} %bitcast.5, bf16[1024,256]{1,0:T(8,128)(2,1)} %bitcast.3, bf16[512,8192]{1,0:T(8,128)(2,1)} %refs_4_.1), custom_call_target="tpu_custom_call" | custom-call | tf_op jit(solution)/shard_map/pallas_call | solution.py:545
  89.4 0.0 copy-done.1
  89.4 0.0 copy-start.2
  89.4 1.5 %fusion = (f32[48]{0:T(128)S(1)}, bf16[48,8192]{1,0:T(8,128)(2,1)S(1)}) fusion(bf16[48,8192]{1,0:T(8,128)(2,1)} %shard_map.86, bf16[48,8192]{1,0:T(8,128)(2,1)S(1)} %copy-done.1), kind=kLoop, calls=%fused_computation.2 | loop fusion | flops 2752464 | bytes 2359488 | tf_op jit(solution)/shard_map/reduce_sum | solution.py:603
  90.9 0.0 copy-start
  91.0 0.0 copy-done.2
  91.0 1.1 %fusion.2 = bf16[48,8192]{1,0:T(8,128)(2,1)} fusion(bf16[48,8192]{1,0:T(8,128)(2,1)S(1)} %get-tuple-element.3, f32[8192]{0:T(1024)S(1)} %copy-done.2, f32[48]{0:T(128)S(1)} %add_sqrt_fusion), kind=kLoop, calls=%fused_computation.4 | loop fusion | flops 1572864 | bytes 1605824 | tf_op jit(solution)/shard_map/convert_element_type | solution.py:604
  92.1 0.0 copy-done
  (1 shorter events, 0.0 us)
Async XLA Ops:
  0.6 88.8 %copy-start.1 = (bf16[48,8192]{1,0:T(8,128)(2,1)S(1)}, bf16[48,8192]{1,0:T(8,128)(2,1)}, u32[]{:S(2)}) copy-start(bf16[48,8192]{1,0:T(8,128)(2,1)} %param.11) | copy-start | bytes 2359300
  89.4 1.6 %copy-start.2 = (f32[8192]{0:T(1024)S(1)}, f32[8192]{0:T(1024)}, u32[]{:S(2)}) copy-start(f32[8192]{0:T(1024)} %param.13) | copy-start | bytes 98308
  90.9 1.2 %copy-start = (bf16[48,8192]{1,0:T(8,128)(2,1)}, bf16[48,8192]{1,0:T(8,128)(2,1)S(1)}, u32[]{:S(2)}) copy-start(bf16[48,8192]{1,0:T(8,128)(2,1)S(1)} %get-tuple-element.3) | copy-start | bytes 2359300

commit v9 on v8

--- a/solution.py
+++ b/solution.py
@@ -251,50 +251,50 @@
 START_RING, START_PAIR, RING_STEP, RING_END, PAIR_STEP, PAIR_RING = range(6)
 ORDER = (
     (START_RING, 4, 0),
-    (START_RING, 1, 0),
+    (START_RING, 3, 0),
     (START_PAIR, 3, 0),
-    (START_RING, 3, 0),
-    (START_PAIR, 0, 0),
-    (START_PAIR, 1, 0),
-    (RING_STEP, 1, 0),
-    (PAIR_STEP, 3, 0),
     (START_RING, 0, 0),
     (RING_STEP, 4, 0),
-    (RING_STEP, 3, 0),
-    (RING_STEP, 1, 1),
-    (PAIR_RING, 3, 0),
     (START_PAIR, 2, 0),
     (START_RING, 2, 0),
+    (PAIR_STEP, 3, 0),
+    (RING_STEP, 3, 0),
     (RING_STEP, 0, 0),
+    (RING_STEP, 4, 1),
+    (START_PAIR, 1, 0),
+    (START_RING, 1, 0),
+    (RING_STEP, 2, 0),
+    (PAIR_RING, 3, 0),
+    (START_PAIR, 0, 0),
+    (PAIR_STEP, 2, 0),
+    (RING_STEP, 3, 1),
+    (RING_STEP, 0, 1),
+    (RING_STEP, 4, 2),
+    (RING_STEP, 1, 0),
+    (RING_STEP, 2, 1),
+    (PAIR_STEP, 1, 0),
+    (PAIR_RING, 3, 1),
+    (PAIR_RING, 2, 0),
+    (RING_STEP, 3, 2),
+    (RING_STEP, 0, 2),
+    (RING_STEP, 1, 1),
+    (RING_STEP, 2, 2),
     (PAIR_STEP, 0, 0),
-    (RING_STEP, 4, 1),
-    (RING_STEP, 3, 1),
+    (PAIR_RING, 1, 0),
+    (PAIR_RING, 3, 2),
+    (PAIR_RING, 2, 1),
+    (RING_END, 4, 0),
     (RING_STEP, 1, 2),
-    (PAIR_RING, 3, 1),
-    (RING_STEP, 0, 1),
-    (RING_STEP, 2, 0),
-    (PAIR_STEP, 1, 0),
-    (RING_STEP, 4, 2),
+    (RING_END, 3, 0),
     (PAIR_RING, 0, 0),
-    (RING_STEP, 3, 2),
-    (PAIR_RING, 3, 2),
-    (RING_STEP, 0, 2),
-    (RING_STEP, 2, 1),
-    (PAIR_STEP, 2, 0),
-    (PAIR_RING, 1, 0),
+    (PAIR_RING, 1, 1),
+    (RING_END, 0, 0),
+    (PAIR_RING, 2, 2),
     (PAIR_RING, 0, 1),
+    (RING_END, 2, 0),
+    (PAIR_RING, 1, 2),
     (RING_END, 1, 0),
-    (RING_STEP, 2, 2),
-    (RING_END, 4, 0),
-    (PAIR_RING, 2, 0),
-    (PAIR_RING, 1, 1),
-    (RING_END, 3, 0),
     (PAIR_RING, 0, 2),
-    (PAIR_RING, 2, 1),
-    (RING_END, 0, 0),
-    (PAIR_RING, 1, 2),
-    (RING_END, 2, 0),
-    (PAIR_RING, 2, 2),
 )
 
 

time: 93 us -> 92.1 us (level)
  no operation moved by 1% of the time
where the time goes in v9:
time: 92.1 us; the launch traced here: 91.3 us
  Pallas kernels  88 us (96%)
  other arithmetic  2.66 us (3%)
    pallas_call x1, Pallas kernels, attend_and_project(): pl.pallas_call(functools.partial(kernel, heads), in_specs=[pl.BlockSpec(m...  88 us

profile of v9, /device:TPU:1, one launch (start us, length us, event | category | flops | bytes accessed | tf_op | source)
XLA Modules:
  0.0 91.3 jit_solution(2469993917553788304)
XLA Ops:
  0.6 0.0 copy-start.1
  0.6 88.0 %shard_map.86 = bf16[48,8192]{1,0:T(8,128)(2,1)} custom-call(s32[32]{0:T(128)} %refs_0_.1, bf16[32,48,128]{2,1,0:T(8,128)(2,1)} %bitcast.4, bf16[384,256]{1,0:T(8,128)(2,1)} %bitcast.5, bf16[1024,256]{1,0:T(8,128)(2,1)} %bitcast.3, bf16[512,8192]{1,0:T(8,128)(2,1)} %refs_4_.1), custom_call_target="tpu_custom_call" | custom-call | tf_op jit(solution)/shard_map/pallas_call | solution.py:545
  88.6 0.0 copy-done.1
  88.6 0.0 copy-start.2
  88.7 1.5 %fusion = (f32[48]{0:T(128)S(1)}, bf16[48,8192]{1,0:T(8,128)(2,1)S(1)}) fusion(bf16[48,8192]{1,0:T(8,128)(2,1)} %shard_map.86, bf16[48,8192]{1,0:T(8,128)(2,1)S(1)} %copy-done.1), kind=kLoop, calls=%fused_computation.2 | loop fusion | flops 2752464 | bytes 2359488 | tf_op jit(solution)/shard_map/reduce_sum | solution.py:603
  90.2 0.0 copy-start
  90.2 0.0 copy-done.2
  90.2 1.1 %fusion.2 = bf16[48,8192]{1,0:T(8,128)(2,1)} fusion(bf16[48,8192]{1,0:T(8,128)(2,1)S(1)} %get-tuple-element.3, f32[8192]{0:T(1024)S(1)} %copy-done.2, f32[48]{0:T(128)S(1)} %add_sqrt_fusion), kind=kLoop, calls=%fused_computation.4 | loop fusion | flops 1572864 | bytes 1605824 | tf_op jit(solution)/shard_map/convert_element_type | solution.py:604
  91.3 0.0 copy-done
  (1 shorter events, 0.0 us)
Async XLA Ops:
  0.6 88.0 %copy-start.1 = (bf16[48,8192]{1,0:T(8,128)(2,1)S(1)}, bf16[48,8192]{1,0:T(8,128)(2,1)}, u32[]{:S(2)}) copy-start(bf16[48,8192]{1,0:T(8,128)(2,1)} %param.11) | copy-start | bytes 2359300
  88.6 1.6 %copy-start.2 = (f32[8192]{0:T(1024)S(1)}, f32[8192]{0:T(1024)}, u32[]{:S(2)}) copy-start(f32[8192]{0:T(1024)} %param.13) | copy-start | bytes 98308
  90.2 1.2 %copy-start = (bf16[48,8192]{1,0:T(8,128)(2,1)}, bf16[48,8192]{1,0:T(8,128)(2,1)S(1)}, u32[]{:S(2)}) copy-start(bf16[48,8192]{1,0:T(8,128)(2,1)S(1)} %get-tuple-element.3) | copy-start | bytes 2359300
